TPU v7x, 32 devices: a whole 2x2x4 slice. The times are simulated.
32 devices in a mesh: groups: 2 (over y), ctx: 4 (over z), kv: 2 (over x), khalf: 2 (over core).
Axes of the slice: x: 2, y: 2, z: 4, core: 2. Of those that a mesh axis runs over, the one named last changes fastest.
Arguments:
- queries: bfloat16 [256, 8192], P(('groups', 'ctx'), 'kv'), parts along dimension 0, may hold values from -100 to 100
- cache_keys: bfloat16 [49152, 1024], P(('groups', 'ctx', 'khalf'), 'kv'), parts along dimension 0, may hold values from -7 to 7
- cache_values: bfloat16 [49152, 1024], P(('groups', 'ctx', 'khalf'), 'kv'), parts along dimension 0, may hold values from -6 to 6
- new_keys: bfloat16 [256, 1024], P(('groups', 'ctx'), 'kv'), parts along dimension 0, may hold values from -10 to 10
- new_values: bfloat16 [256, 1024], P(('groups', 'ctx'), 'kv'), parts along dimension 0, may hold values from -6 to 6
- cache_blocks: int32 [2], P('groups'), parts along dimension 0, may hold values from 48 to 192
- residual: bfloat16 [256, 8192], P('groups', ('ctx', 'khalf')), parts along dimension 0, may hold values from -20 to 20
- norm_gain: float32 [8192], P(('ctx', 'khalf')), may hold values from 0.1 to 1.9
- out_weight: bfloat16 [8192, 8192], P('kv', ('ctx', 'khalf')), may hold values from -0.0625 to 0.0625
- gate_up: bfloat16 [8192, 2, 14336], P(('ctx', 'khalf'), None, 'kv'), may hold values from -0.0625 to 0.0625
- down_weight: bfloat16 [14336, 8192], P('kv', ('ctx', 'khalf')), may hold values from -0.046875 to 0.046875
Outputs:
- layer_out: bfloat16 [256, 8192], P(('groups', 'kv'), ('ctx', 'khalf')), parts along dimension 0
There are 2 independent parts, one for each index of `groups`. A program takes and returns all parts, laid end to end along the dimension named above; an argument that names none is the same for every part. Nothing has to cross between parts.
Inputs may be any that keep to these rules, and one draw needn't show every extreme that they name: The first 128 * cache_blocks[0] cached positions are valid.
All inputs are finite; a program needn't handle non-finite values.
Results may differ from a plain program's by a relative error of at most 0.019.
Values may be sent and summed in bfloat16 or wider, within the bound.
A program may use at most 128 MiB of HBM per device.

v0:
```python
import jax
import jax.numpy as jnp
from jax import lax
from jax.sharding import PartitionSpec as P

D = 8192
HQ = 64
KVH = 8
DH = 128
BLOCK = 128


NEG = -1e30
EPSILON = 1e-05


def shifted(value, axis, by):
    devices = lax.axis_size(axis)
    return lax.ppermute(value, axis, [(i, (i + by) % devices) for i in range(devices)])


def merged_2(value, axis, combine):
    everything = jax.tree.map(
        lambda part, kind: lax.all_gather(part.astype(kind), axis),
        value,
        jax.tree.map(lambda a: jnp.bfloat16 if a.dtype == jnp.float32 else a.dtype, value),
    )

    def take(k):
        return jax.tree.map(lambda part, own: part[k].astype(own.dtype), everything, value)

    return lax.fori_loop(
        1, lax.axis_size(axis), lambda k, so_far: combine(so_far, take(k)), take(0)
    )


def attend(query_block, key_block, value_block, allowed):
    row_count, local_groups, group_size, head_width = query_block.shape
    key_count = key_block.shape[0]
    keyed = key_block.reshape(key_count, local_groups, head_width)
    valued = value_block.reshape(key_count, local_groups, head_width)
    scores = jnp.einsum(
        "rkgd,nkd->rkgn", query_block, keyed, preferred_element_type=jnp.float32
    ) * head_width ** (-0.5)
    usable = allowed[:, None, None, :]
    scores = jnp.where(usable, scores, NEG)
    peak_score = jnp.max(scores, axis=3)
    weights = jnp.where(usable, jnp.exp(scores - peak_score[..., None]), 0.0)
    weight_sum = jnp.sum(weights, axis=3)
    summed = jnp.einsum(
        "rkgn,nkd->rkgd", weights.astype(jnp.bfloat16), valued, preferred_element_type=jnp.float32
    )
    return (summed, peak_score, weight_sum)


def combine(earlier_part, later_part):
    earlier_sum, earlier_peak, earlier_total = earlier_part
    later_sum, later_peak, later_total = later_part
    new_peak = jnp.maximum(earlier_peak, later_peak)
    earlier_scale = jnp.exp(earlier_peak - new_peak)
    later_scale = jnp.exp(later_peak - new_peak)
    return (
        earlier_sum * earlier_scale[..., None] + later_sum * later_scale[..., None],
        new_peak,
        earlier_total * earlier_scale + later_total * later_scale,
    )


def normalize(hidden_state, norm_gain):
    values32 = hidden_state.astype(jnp.float32)
    squares = lax.psum(jnp.sum(values32 * values32, axis=1), ("ctx", "khalf"))
    factor = lax.rsqrt(squares / D + EPSILON)
    return (values32 * factor[:, None] * norm_gain).astype(jnp.bfloat16)


def on_device(
    queries,
    cache_keys,
    cache_values,
    new_keys,
    new_values,
    cache_blocks,
    residual,
    norm_gain,
    out_weight,
    gate_up,
    down_weight,
):
    query_rows = queries.shape[0]
    group_size = HQ // KVH
    local_groups = cache_keys.shape[1] // DH
    local_queries = queries.reshape(query_rows, local_groups, group_size, DH)
    cache_length = cache_keys.shape[0]
    shard_index = lax.axis_index("ctx") * lax.axis_size("khalf") + lax.axis_index("khalf")
    positions = shard_index * cache_length + jnp.arange(cache_length, dtype=jnp.int32)
    cache_allowed = (positions < cache_blocks[0] * BLOCK)[None, :]
    query_start = lax.axis_index("ctx") * query_rows
    query_positions = query_start + jnp.arange(query_rows, dtype=jnp.int32)
    empty = (
        jnp.zeros((query_rows, local_groups, group_size, DH), jnp.float32),
        jnp.full((query_rows, local_groups, group_size), NEG, jnp.float32),
        jnp.zeros((query_rows, local_groups, group_size), jnp.float32),
    )

    def cycle_step(step_index, state_carry):
        visiting, partial_state = state_carry
        fresh = attend(visiting, cache_keys, cache_values, cache_allowed)
        partial_state = combine(partial_state, fresh)
        visiting = shifted(visiting, "ctx", 1)
        partial_state = (
            shifted(partial_state[0].astype(jnp.bfloat16), "ctx", 1).astype(jnp.float32),
            shifted(partial_state[1].astype(jnp.bfloat16), "ctx", 1).astype(jnp.float32),
            shifted(partial_state[2].astype(jnp.bfloat16), "ctx", 1).astype(jnp.float32),
        )
        return (visiting, partial_state)

    returned, cache_part = lax.fori_loop(
        0, lax.axis_size("ctx"), cycle_step, (local_queries, empty)
    )
    merged = merged_2(cache_part, "khalf", combine)
    piece_keys = lax.all_gather(new_keys, "ctx", axis=0, tiled=True)
    piece_values = lax.all_gather(new_values, "ctx", axis=0, tiled=True)
    key_positions = jnp.arange(piece_keys.shape[0], dtype=jnp.int32)
    allowed = key_positions[None, :] <= query_positions[:, None]
    own_part = combine(empty, attend(local_queries, piece_keys, piece_values, allowed))
    joined = combine(merged, own_part)
    attention = (
        (joined[0] / joined[2][..., None])
        .astype(jnp.bfloat16)
        .reshape(query_rows, local_groups * group_size * DH)
    )
    partial_rows = jnp.dot(
        lax.all_gather(attention, "ctx", axis=0, tiled=True),
        out_weight,
        preferred_element_type=jnp.float32,
    )
    projected = lax.psum(partial_rows.astype(jnp.bfloat16), "kv").astype(jnp.float32)
    hidden_state = (residual.astype(jnp.float32) + projected).astype(jnp.bfloat16)
    normed = normalize(hidden_state, norm_gain)
    own_rows = hidden_state.shape[0] // lax.axis_size("kv")
    kept = lax.dynamic_slice_in_dim(hidden_state, lax.axis_index("kv") * own_rows, own_rows, 0)
    local_width = gate_up.shape[0]
    local_hidden = gate_up.shape[2]
    merged_weight = gate_up.reshape(local_width, 2 * local_hidden)
    both = lax.psum_scatter(
        jnp.dot(normed, merged_weight, preferred_element_type=jnp.float32).astype(jnp.bfloat16),
        ("ctx", "khalf"),
        scatter_dimension=0,
        tiled=True,
    ).astype(jnp.float32)
    activated = (jax.nn.silu(both[:, :local_hidden]) * both[:, local_hidden:]).astype(jnp.bfloat16)
    partial_out = jnp.dot(
        lax.all_gather(activated, ("ctx", "khalf"), axis=0, tiled=True),
        down_weight,
        preferred_element_type=jnp.float32,
    )
    down = lax.psum_scatter(
        partial_out.astype(jnp.bfloat16), "kv", scatter_dimension=0, tiled=True
    ).astype(jnp.float32)
    return (kept.astype(jnp.float32) + down).astype(jnp.bfloat16)


def solution(mesh):
    in_specs = (
        P(("groups", "ctx"), "kv"),
        P(("groups", "ctx", "khalf"), "kv"),
        P(("groups", "ctx", "khalf"), "kv"),
        P(("groups", "ctx"), "kv"),
        P(("groups", "ctx"), "kv"),
        P("groups"),
        P("groups", ("ctx", "khalf")),
        P(("ctx", "khalf")),
        P("kv", ("ctx", "khalf")),
        P(("ctx", "khalf"), None, "kv"),
        P("kv", ("ctx", "khalf")),
    )
    out_specs = P(("groups", "kv"), ("ctx", "khalf"))
    return jax.shard_map(
        on_device, mesh=mesh, in_specs=in_specs, out_specs=out_specs, check_vma=False
    )
```

profile of v0, /device:TPU:0, one launch (start us, length us, event | category | flops | bytes accessed | tf_op | source)
XLA Modules:
  0.0 343.9 jit_solution(14457301337090552789)
XLA Ops:
  7.3 15.3 %all_gather.34 = bf16[128,512]{1,0:T(8,128)(2,1)S(1)} all-gather(bf16[32,512]{1,0:T(8,128)(2,1)} %param.16), channel_id=1, replica_groups=mesh['groups'=2,'ctx'=4,'kv'=2,'khalf'=2] {'ctx'}, dimensions={0}, use_global_device_ids=true | all-gather | bytes 163840 | tf_op jit(solution)/shard_map/all_gather | solution.py:121
  22.7 13.7 %all_gather.35 = bf16[128,512]{1,0:T(8,128)(2,1)S(1)} all-gather(bf16[32,512]{1,0:T(8,128)(2,1)} %param.17), channel_id=1, replica_groups=mesh['groups'=2,'ctx'=4,'kv'=2,'khalf'=2] {'ctx'}, dimensions={0}, use_global_device_ids=true | all-gather | bytes 163840 | tf_op jit(solution)/shard_map/all_gather | solution.py:122
  37.6 5.5 %reshape.182 = bf16[3072,4,128]{2,1,0:T(4,128)(2,1)} reshape(bf16[3072,512]{1,0:T(8,128)(2,1)} %param.14) | data formatting | bytes 6291456 | tf_op jit(solution)/shard_map/while/body/eval_jaxpr/reshape | solution.py:40
  43.1 5.5 %reshape.181 = bf16[3072,4,128]{2,1,0:T(4,128)(2,1)} reshape(bf16[3072,512]{1,0:T(8,128)(2,1)} %param.15) | data formatting | bytes 6291456 | tf_op jit(solution)/shard_map/while/body/eval_jaxpr/reshape | solution.py:41
  48.6 100.1 %while.4 = (s32[]{:T(128)}, bf16[32,4,8,128]{3,0,2,1:T(8,128)(2,1)S(1)}, f32[32,4,8,128]{3,0,2,1:T(8,128)S(1)}, f32[32,4,8]{0,2,1:T(8,128)S(1)}, f32[32,4,8]{0,2...) while((s32[]{:T(128)}, ...), condition=%wide.wide.region_3.4_spmd.clone, body=%wide.wide.region_0.3_spmd.clone.sunk | while | flops 1652313088 | bytes 48599340 | solution.py:117
  48.7 4.4 %bitcast_reduce_fusion.3 = (f32[32,4,8]{0,2,1:T(8,128)S(1)}, f32[4,3072,32,8]{1,2,3,0:T(8,128)S(1)}) fusion(pred[3072]{0:T(1024)(128)(4,1)S(1)} %add_compare_fusion.3, bf16[32,4,8,128]{3,0,2,1:T(8,128)(2,1)S(1)} %copy.169, bf16[3072,4,128,1]{2,1,0,3:T(4,128)(2,1)} %bitcast.100), kind=kOutput, calls=%fused_computation.2.clone.clone.1 | convolution fusion | flops 814742528 | bytes 15997952 | tf_op jit(solution)/shard_map/while/body/eval_jaxpr/rkgd,nkd->rkgn/dot_general | solution.py:42
  53.1 3.6 %fusion.100 = f32[32,4,8]{0,2,1:T(8,128)S(1)} fusion(f32[4,3072,32,8]{1,2,3,0:T(8,128)S(1)} %get-tuple-element.298, f32[32,4,8]{0,2,1:T(8,128)S(1)} %get-tuple-element.299, pred[3072]{0:T(1024)(128)(4,1)S(1)} %add_compare_fusion.3), kind=kLoop, calls=%fused_computation.6.clone.clone.1 | loop fusion | flops 15727616 | bytes 12594176 | tf_op jit(solution)/shard_map/while/body/eval_jaxpr/reduce_sum | solution.py:49
  56.7 5.6 %fusion.102 = bf16[32,4,8,128]{3,0,2,1:T(8,128)(2,1)S(1)} fusion(bf16[3072,4,128,1]{2,1,0,3:T(4,128)(2,1)} %bitcast.101, f32[4,3072,32,8]{1,2,3,0:T(8,128)S(1)} %get-tuple-element.298, f32[32,4,8]{0,2,1:T(8,128)S(1)} %get-tuple-element.299, pred[3072]{0:T(1024)(128)(4,1)S(1)} %add_compare_fusion.3, ...), kind=kOutput, calls=%fused_computation.17.clone.clone.1 | convolution fusion | flops 821690368 | bytes 16530433 | tf_op jit(solution)/shard_map/while/body/eval_jaxpr/rkgn,nkd->rkgd/dot_general | solution.py:50
  67.4 6.1 %collective-permute-done.2 = bf16[32,4,8]{0,2,1:T(8,128)(2,1)S(1)} collective-permute-done((bf16[32,4,8]{0,2,1:T(8,128)(2,1)S(1)}, bf16[32,4,8]{0,2,1:T(8,128)(2,1)S(1)}, u32[]{:S(2)}, u32[]{:S(2)}) %collective-permute-start.2) | collective-permute-done | bytes 2080 | tf_op jit(solution)/shard_map/while/body/eval_jaxpr/ppermute | solution.py:19
  73.7 4.4 %bitcast_reduce_fusion.3 = (f32[32,4,8]{0,2,1:T(8,128)S(1)}, f32[4,3072,32,8]{1,2,3,0:T(8,128)S(1)}) fusion(pred[3072]{0:T(1024)(128)(4,1)S(1)} %add_compare_fusion.3, bf16[32,4,8,128]{3,0,2,1:T(8,128)(2,1)S(1)} %copy.169, bf16[3072,4,128,1]{2,1,0,3:T(4,128)(2,1)} %bitcast.100), kind=kOutput, calls=%fused_computation.2.clone.clone.1 | convolution fusion | flops 814742528 | bytes 15997952 | tf_op jit(solution)/shard_map/while/body/eval_jaxpr/rkgd,nkd->rkgn/dot_general | solution.py:42
  78.2 3.6 %fusion.100 = f32[32,4,8]{0,2,1:T(8,128)S(1)} fusion(f32[4,3072,32,8]{1,2,3,0:T(8,128)S(1)} %get-tuple-element.298, f32[32,4,8]{0,2,1:T(8,128)S(1)} %get-tuple-element.299, pred[3072]{0:T(1024)(128)(4,1)S(1)} %add_compare_fusion.3), kind=kLoop, calls=%fused_computation.6.clone.clone.1 | loop fusion | flops 15727616 | bytes 12594176 | tf_op jit(solution)/shard_map/while/body/eval_jaxpr/reduce_sum | solution.py:49
  81.8 5.6 %fusion.102 = bf16[32,4,8,128]{3,0,2,1:T(8,128)(2,1)S(1)} fusion(bf16[3072,4,128,1]{2,1,0,3:T(4,128)(2,1)} %bitcast.101, f32[4,3072,32,8]{1,2,3,0:T(8,128)S(1)} %get-tuple-element.298, f32[32,4,8]{0,2,1:T(8,128)S(1)} %get-tuple-element.299, pred[3072]{0:T(1024)(128)(4,1)S(1)} %add_compare_fusion.3, ...), kind=kOutput, calls=%fused_computation.17.clone.clone.1 | convolution fusion | flops 821690368 | bytes 16530433 | tf_op jit(solution)/shard_map/while/body/eval_jaxpr/rkgn,nkd->rkgd/dot_general | solution.py:50
  92.4 6.1 %collective-permute-done.2 = bf16[32,4,8]{0,2,1:T(8,128)(2,1)S(1)} collective-permute-done((bf16[32,4,8]{0,2,1:T(8,128)(2,1)S(1)}, bf16[32,4,8]{0,2,1:T(8,128)(2,1)S(1)}, u32[]{:S(2)}, u32[]{:S(2)}) %collective-permute-start.2) | collective-permute-done | bytes 2080 | tf_op jit(solution)/shard_map/while/body/eval_jaxpr/ppermute | solution.py:19
  98.7 4.4 %bitcast_reduce_fusion.3 = (f32[32,4,8]{0,2,1:T(8,128)S(1)}, f32[4,3072,32,8]{1,2,3,0:T(8,128)S(1)}) fusion(pred[3072]{0:T(1024)(128)(4,1)S(1)} %add_compare_fusion.3, bf16[32,4,8,128]{3,0,2,1:T(8,128)(2,1)S(1)} %copy.169, bf16[3072,4,128,1]{2,1,0,3:T(4,128)(2,1)} %bitcast.100), kind=kOutput, calls=%fused_computation.2.clone.clone.1 | convolution fusion | flops 814742528 | bytes 15997952 | tf_op jit(solution)/shard_map/while/body/eval_jaxpr/rkgd,nkd->rkgn/dot_general | solution.py:42
  103.2 3.6 %fusion.100 = f32[32,4,8]{0,2,1:T(8,128)S(1)} fusion(f32[4,3072,32,8]{1,2,3,0:T(8,128)S(1)} %get-tuple-element.298, f32[32,4,8]{0,2,1:T(8,128)S(1)} %get-tuple-element.299, pred[3072]{0:T(1024)(128)(4,1)S(1)} %add_compare_fusion.3), kind=kLoop, calls=%fused_computation.6.clone.clone.1 | loop fusion | flops 15727616 | bytes 12594176 | tf_op jit(solution)/shard_map/while/body/eval_jaxpr/reduce_sum | solution.py:49
  106.8 5.6 %fusion.102 = bf16[32,4,8,128]{3,0,2,1:T(8,128)(2,1)S(1)} fusion(bf16[3072,4,128,1]{2,1,0,3:T(4,128)(2,1)} %bitcast.101, f32[4,3072,32,8]{1,2,3,0:T(8,128)S(1)} %get-tuple-element.298, f32[32,4,8]{0,2,1:T(8,128)S(1)} %get-tuple-element.299, pred[3072]{0:T(1024)(128)(4,1)S(1)} %add_compare_fusion.3, ...), kind=kOutput, calls=%fused_computation.17.clone.clone.1 | convolution fusion | flops 821690368 | bytes 16530433 | tf_op jit(solution)/shard_map/while/body/eval_jaxpr/rkgn,nkd->rkgd/dot_general | solution.py:50
  113.6 3.8 %collective-permute-start.3 = (bf16[32,4,8]{0,2,1:T(8,128)(2,1)S(1)}, bf16[32,4,8]{0,2,1:T(8,128)(2,1)S(1)}, u32[]{:S(2)}, u32[]{:S(2)}) collective-permute-start(bf16[32,4,8]{0,2,1:T(8,128)(2,1)S(1)} %get-tuple-element.302), channel_id=1, source_target_pairs={{0,4},{4,8},{8,12},{12,0},{1,5},{5,9},{9,13},{13,1},{2,6},{6,10},{... | collective-permute-start | bytes 6152 | tf_op jit(solution)/shard_map/while/body/eval_jaxpr/ppermute | solution.py:19
  117.4 6.1 %collective-permute-done.2 = bf16[32,4,8]{0,2,1:T(8,128)(2,1)S(1)} collective-permute-done((bf16[32,4,8]{0,2,1:T(8,128)(2,1)S(1)}, bf16[32,4,8]{0,2,1:T(8,128)(2,1)S(1)}, u32[]{:S(2)}, u32[]{:S(2)}) %collective-permute-start.2) | collective-permute-done | bytes 2080 | tf_op jit(solution)/shard_map/while/body/eval_jaxpr/ppermute | solution.py:19
  123.7 4.4 %bitcast_reduce_fusion.3 = (f32[32,4,8]{0,2,1:T(8,128)S(1)}, f32[4,3072,32,8]{1,2,3,0:T(8,128)S(1)}) fusion(pred[3072]{0:T(1024)(128)(4,1)S(1)} %add_compare_fusion.3, bf16[32,4,8,128]{3,0,2,1:T(8,128)(2,1)S(1)} %copy.169, bf16[3072,4,128,1]{2,1,0,3:T(4,128)(2,1)} %bitcast.100), kind=kOutput, calls=%fused_computation.2.clone.clone.1 | convolution fusion | flops 814742528 | bytes 15997952 | tf_op jit(solution)/shard_map/while/body/eval_jaxpr/rkgd,nkd->rkgn/dot_general | solution.py:42
  128.2 3.6 %fusion.100 = f32[32,4,8]{0,2,1:T(8,128)S(1)} fusion(f32[4,3072,32,8]{1,2,3,0:T(8,128)S(1)} %get-tuple-element.298, f32[32,4,8]{0,2,1:T(8,128)S(1)} %get-tuple-element.299, pred[3072]{0:T(1024)(128)(4,1)S(1)} %add_compare_fusion.3), kind=kLoop, calls=%fused_computation.6.clone.clone.1 | loop fusion | flops 15727616 | bytes 12594176 | tf_op jit(solution)/shard_map/while/body/eval_jaxpr/reduce_sum | solution.py:49
  131.8 5.6 %fusion.102 = bf16[32,4,8,128]{3,0,2,1:T(8,128)(2,1)S(1)} fusion(bf16[3072,4,128,1]{2,1,0,3:T(4,128)(2,1)} %bitcast.101, f32[4,3072,32,8]{1,2,3,0:T(8,128)S(1)} %get-tuple-element.298, f32[32,4,8]{0,2,1:T(8,128)S(1)} %get-tuple-element.299, pred[3072]{0:T(1024)(128)(4,1)S(1)} %add_compare_fusion.3, ...), kind=kOutput, calls=%fused_computation.17.clone.clone.1 | convolution fusion | flops 821690368 | bytes 16530433 | tf_op jit(solution)/shard_map/while/body/eval_jaxpr/rkgn,nkd->rkgd/dot_general | solution.py:50
  138.2 4.3 %collective-permute-start.3 = (bf16[32,4,8]{0,2,1:T(8,128)(2,1)S(1)}, bf16[32,4,8]{0,2,1:T(8,128)(2,1)S(1)}, u32[]{:S(2)}, u32[]{:S(2)}) collective-permute-start(bf16[32,4,8]{0,2,1:T(8,128)(2,1)S(1)} %get-tuple-element.302), channel_id=1, source_target_pairs={{0,4},{4,8},{8,12},{12,0},{1,5},{5,9},{9,13},{13,1},{2,6},{6,10},{... | collective-permute-start | bytes 6152 | tf_op jit(solution)/shard_map/while/body/eval_jaxpr/ppermute | solution.py:19
  142.4 6.1 %collective-permute-done.2 = bf16[32,4,8]{0,2,1:T(8,128)(2,1)S(1)} collective-permute-done((bf16[32,4,8]{0,2,1:T(8,128)(2,1)S(1)}, bf16[32,4,8]{0,2,1:T(8,128)(2,1)S(1)}, u32[]{:S(2)}, u32[]{:S(2)}) %collective-permute-start.2) | collective-permute-done | bytes 2080 | tf_op jit(solution)/shard_map/while/body/eval_jaxpr/ppermute | solution.py:19
  159.0 26.3 %all-gather.6.cloned.1.call-done = bf16[128,4096]{1,0:T(8,128)(2,1)} async-done(((bf16[32,4096]{1,0:T(8,128)(2,1)}), bf16[128,4096]{1,0:T(8,128)(2,1)}) %all-gather.6.cloned.1.call-update) | async-done | bytes 1048592 | tf_op jit(solution)/shard_map/all_gather | solution.py:133
  185.3 5.7 %convolution_convert_fusion.1 = bf16[128,1024]{1,0:T(8,128)(2,1)} fusion(bf16[128,4096]{1,0:T(8,128)(2,1)} %all-gather.6.cloned.1.call-done, bf16[4096,1024]{1,0:T(8,128)(2,1)} %param.21), kind=kOutput, calls=%fused_computation.40 | convolution fusion | flops 1073872896 | bytes 9699328 | tf_op jit(solution)/shard_map/dot_general | solution.py:132
  191.2 20.5 %copy.132 = bf16[128,8,2,7168]{3,1,2,0:T(8,128)(2,1)} copy(bf16[128,8,2,7168]{3,2,1,0:T(2,128)(2,1)} %bitcast.99) | data formatting | bytes 58720256
  214.9 15.9 %psum.15 = f32[128]{0:T(128)S(1)} all-reduce(f32[128]{0:T(128)S(1)} %get-tuple-element.167), channel_id=1, replica_groups=mesh['groups'=2,'ctx'=4,'kv'=2,'khalf'=2] {'ctx','khalf'}, use_global_device_ids=true, to_apply=%region_8.9 | all-reduce | flops 128 | bytes 1024 | tf_op jit(solution)/shard_map/psum | solution.py:71
  230.8 15.2 %convolution_convert_fusion = bf16[128,14336]{1,0:T(8,128)(2,1)} fusion(bf16[1024,14336]{1,0:T(8,128)(2,1)} %bitcast.98, bf16[128,1024]{1,0:T(8,128)(2,1)S(1)} %get-tuple-element.168, f32[1024]{0:T(1024)S(1)} %copy-done.1, f32[128]{0:T(128)S(1)} %add_rsqrt_fusion), kind=kOutput, calls=%fused_computation.30 | convolution fusion | flops 3760455680 | bytes 33296896 | tf_op jit(solution)/shard_map/dot_general | solution.py:146
  246.1 42.4 %reduce-scatter.3.cloned.1.call-done = bf16[16,14336]{1,0:T(8,128)(2,1)} async-done(((bf16[128,14336]{1,0:T(8,128)(2,1)}), bf16[16,14336]{1,0:T(8,128)(2,1)}) %reduce-scatter.3.cloned.1.call-update) | async-done | bytes 458768 | tf_op jit(solution)/shard_map/reduce_scatter | solution.py:145
  290.5 25.4 %all-gather.8.cloned.1.call-done = bf16[128,7168]{1,0:T(8,128)(2,1)} async-done(((bf16[16,7168]{1,0:T(8,128)(2,1)}), bf16[128,7168]{1,0:T(8,128)(2,1)}) %all-gather.8.cloned.1.call-update) | async-done | bytes 1835024 | tf_op jit(solution)/shard_map/all_gather | solution.py:153
  315.9 8.5 %convolution_convert_fusion.2 = bf16[128,1024]{1,0:T(8,128)(2,1)} fusion(bf16[128,7168]{1,0:T(8,128)(2,1)} %all-gather.8.cloned.1.call-done, bf16[7168,1024]{1,0:T(8,128)(2,1)} %param.23), kind=kOutput, calls=%fused_computation.42 | convolution fusion | flops 1879179264 | bytes 16777216 | tf_op jit(solution)/shard_map/dot_general | solution.py:152
  324.4 11.3 %reduce-scatter.5.cloned.1.call-done = bf16[64,1024]{1,0:T(8,128)(2,1)} async-done(((bf16[128,1024]{1,0:T(8,128)(2,1)}), bf16[64,1024]{1,0:T(8,128)(2,1)}) %reduce-scatter.5.cloned.1.call-update) | async-done | bytes 131088 | tf_op jit(solution)/shard_map/reduce_scatter | solution.py:157
  (110 shorter events, 31.3 us)
Async XLA Ops:
  6.5 178.7 %all-gather.6.cloned.1.call-start = ((), (), s32[]{:S(2)}) async-start(), calls=%async_computation.2 | async-start | bytes 1310720 | tf_op jit(solution)/shard_map/all_gather | solution.py:133
  62.4 11.2 %collective-permute-start.1 = (bf16[32,4,8,128]{3,0,2,1:T(8,128)(2,1)S(1)}, bf16[32,4,8,128]{3,0,2,1:T(8,128)(2,1)S(1)}, u32[]{:S(2)}, u32[]{:S(2)}) collective-permute-start(bf16[32,4,8,128]{3,0,2,1:T(8,128)(2,1)S(1)} %fusion.102), channel_id=1, source_target_pairs={{0,4},{4,8},{8,12},{12,0},{1,5},{5,9},{9,13},{13,1},{2,6},{6,10},{... | collective-permute-start | bytes 786440 | tf_op jit(solution)/shard_map/while/body/eval_jaxpr/ppermute | solution.py:19
  64.1 9.5 %collective-permute-start = (bf16[32,4,8,128]{3,0,2,1:T(8,128)(2,1)S(1)}, bf16[32,4,8,128]{3,0,2,1:T(8,128)(2,1)S(1)}, u32[]{:S(2)}, u32[]{:S(2)}) collective-permute-start(bf16[32,4,8,128]{3,0,2,1:T(8,128)(2,1)S(1)} %copy.169), channel_id=1, source_target_pairs={{0,4},{4,8},{8,12},{12,0},{1,5},{5,9},{9,13},{13,1},{2,6},{6,10},{... | collective-permute-start | bytes 786440 | tf_op jit(solution)/shard_map/while/body/eval_jaxpr/ppermute | solution.py:19
  64.2 9.3 %collective-permute-start.2 = (bf16[32,4,8]{0,2,1:T(8,128)(2,1)S(1)}, bf16[32,4,8]{0,2,1:T(8,128)(2,1)S(1)}, u32[]{:S(2)}, u32[]{:S(2)}) collective-permute-start(bf16[32,4,8]{0,2,1:T(8,128)(2,1)S(1)} %fusion.103), channel_id=1, source_target_pairs={{0,4},{4,8},{8,12},{12,0},{1,5},{5,9},{9,13},{13,1},{2,6},{6,10},{... | collective-permute-start | bytes 6152 | tf_op jit(solution)/shard_map/while/body/eval_jaxpr/ppermute | solution.py:19
  67.1 6.4 %collective-permute-start.3 = (bf16[32,4,8]{0,2,1:T(8,128)(2,1)S(1)}, bf16[32,4,8]{0,2,1:T(8,128)(2,1)S(1)}, u32[]{:S(2)}, u32[]{:S(2)}) collective-permute-start(bf16[32,4,8]{0,2,1:T(8,128)(2,1)S(1)} %get-tuple-element.302), channel_id=1, source_target_pairs={{0,4},{4,8},{8,12},{12,0},{1,5},{5,9},{9,13},{13,1},{2,6},{6,10},{... | collective-permute-start | bytes 6152 | tf_op jit(solution)/shard_map/while/body/eval_jaxpr/ppermute | solution.py:19
  87.4 11.2 %collective-permute-start.1 = (bf16[32,4,8,128]{3,0,2,1:T(8,128)(2,1)S(1)}, bf16[32,4,8,128]{3,0,2,1:T(8,128)(2,1)S(1)}, u32[]{:S(2)}, u32[]{:S(2)}) collective-permute-start(bf16[32,4,8,128]{3,0,2,1:T(8,128)(2,1)S(1)} %fusion.102), channel_id=1, source_target_pairs={{0,4},{4,8},{8,12},{12,0},{1,5},{5,9},{9,13},{13,1},{2,6},{6,10},{... | collective-permute-start | bytes 786440 | tf_op jit(solution)/shard_map/while/body/eval_jaxpr/ppermute | solution.py:19
  87.4 11.2 %collective-permute-start = (bf16[32,4,8,128]{3,0,2,1:T(8,128)(2,1)S(1)}, bf16[32,4,8,128]{3,0,2,1:T(8,128)(2,1)S(1)}, u32[]{:S(2)}, u32[]{:S(2)}) collective-permute-start(bf16[32,4,8,128]{3,0,2,1:T(8,128)(2,1)S(1)} %copy.169), channel_id=1, source_target_pairs={{0,4},{4,8},{8,12},{12,0},{1,5},{5,9},{9,13},{13,1},{2,6},{6,10},{... | collective-permute-start | bytes 786440 | tf_op jit(solution)/shard_map/while/body/eval_jaxpr/ppermute | solution.py:19
  87.9 10.6 %collective-permute-start.2 = (bf16[32,4,8]{0,2,1:T(8,128)(2,1)S(1)}, bf16[32,4,8]{0,2,1:T(8,128)(2,1)S(1)}, u32[]{:S(2)}, u32[]{:S(2)}) collective-permute-start(bf16[32,4,8]{0,2,1:T(8,128)(2,1)S(1)} %fusion.103), channel_id=1, source_target_pairs={{0,4},{4,8},{8,12},{12,0},{1,5},{5,9},{9,13},{13,1},{2,6},{6,10},{... | collective-permute-start | bytes 6152 | tf_op jit(solution)/shard_map/while/body/eval_jaxpr/ppermute | solution.py:19
  90.3 8.2 %collective-permute-start.3 = (bf16[32,4,8]{0,2,1:T(8,128)(2,1)S(1)}, bf16[32,4,8]{0,2,1:T(8,128)(2,1)S(1)}, u32[]{:S(2)}, u32[]{:S(2)}) collective-permute-start(bf16[32,4,8]{0,2,1:T(8,128)(2,1)S(1)} %get-tuple-element.302), channel_id=1, source_target_pairs={{0,4},{4,8},{8,12},{12,0},{1,5},{5,9},{9,13},{13,1},{2,6},{6,10},{... | collective-permute-start | bytes 6152 | tf_op jit(solution)/shard_map/while/body/eval_jaxpr/ppermute | solution.py:19
  112.4 11.2 %collective-permute-start.1 = (bf16[32,4,8,128]{3,0,2,1:T(8,128)(2,1)S(1)}, bf16[32,4,8,128]{3,0,2,1:T(8,128)(2,1)S(1)}, u32[]{:S(2)}, u32[]{:S(2)}) collective-permute-start(bf16[32,4,8,128]{3,0,2,1:T(8,128)(2,1)S(1)} %fusion.102), channel_id=1, source_target_pairs={{0,4},{4,8},{8,12},{12,0},{1,5},{5,9},{9,13},{13,1},{2,6},{6,10},{... | collective-permute-start | bytes 786440 | tf_op jit(solution)/shard_map/while/body/eval_jaxpr/ppermute | solution.py:19
  112.5 11.2 %collective-permute-start = (bf16[32,4,8,128]{3,0,2,1:T(8,128)(2,1)S(1)}, bf16[32,4,8,128]{3,0,2,1:T(8,128)(2,1)S(1)}, u32[]{:S(2)}, u32[]{:S(2)}) collective-permute-start(bf16[32,4,8,128]{3,0,2,1:T(8,128)(2,1)S(1)} %copy.169), channel_id=1, source_target_pairs={{0,4},{4,8},{8,12},{12,0},{1,5},{5,9},{9,13},{13,1},{2,6},{6,10},{... | collective-permute-start | bytes 786440 | tf_op jit(solution)/shard_map/while/body/eval_jaxpr/ppermute | solution.py:19
  112.5 11.0 %collective-permute-start.2 = (bf16[32,4,8]{0,2,1:T(8,128)(2,1)S(1)}, bf16[32,4,8]{0,2,1:T(8,128)(2,1)S(1)}, u32[]{:S(2)}, u32[]{:S(2)}) collective-permute-start(bf16[32,4,8]{0,2,1:T(8,128)(2,1)S(1)} %fusion.103), channel_id=1, source_target_pairs={{0,4},{4,8},{8,12},{12,0},{1,5},{5,9},{9,13},{13,1},{2,6},{6,10},{... | collective-permute-start | bytes 6152 | tf_op jit(solution)/shard_map/while/body/eval_jaxpr/ppermute | solution.py:19
  113.6 10.0 %collective-permute-start.3 = (bf16[32,4,8]{0,2,1:T(8,128)(2,1)S(1)}, bf16[32,4,8]{0,2,1:T(8,128)(2,1)S(1)}, u32[]{:S(2)}, u32[]{:S(2)}) collective-permute-start(bf16[32,4,8]{0,2,1:T(8,128)(2,1)S(1)} %get-tuple-element.302), channel_id=1, source_target_pairs={{0,4},{4,8},{8,12},{12,0},{1,5},{5,9},{9,13},{13,1},{2,6},{6,10},{... | collective-permute-start | bytes 6152 | tf_op jit(solution)/shard_map/while/body/eval_jaxpr/ppermute | solution.py:19
  137.4 11.2 %collective-permute-start.1 = (bf16[32,4,8,128]{3,0,2,1:T(8,128)(2,1)S(1)}, bf16[32,4,8,128]{3,0,2,1:T(8,128)(2,1)S(1)}, u32[]{:S(2)}, u32[]{:S(2)}) collective-permute-start(bf16[32,4,8,128]{3,0,2,1:T(8,128)(2,1)S(1)} %fusion.102), channel_id=1, source_target_pairs={{0,4},{4,8},{8,12},{12,0},{1,5},{5,9},{9,13},{13,1},{2,6},{6,10},{... | collective-permute-start | bytes 786440 | tf_op jit(solution)/shard_map/while/body/eval_jaxpr/ppermute | solution.py:19
  137.5 11.2 %collective-permute-start = (bf16[32,4,8,128]{3,0,2,1:T(8,128)(2,1)S(1)}, bf16[32,4,8,128]{3,0,2,1:T(8,128)(2,1)S(1)}, u32[]{:S(2)}, u32[]{:S(2)}) collective-permute-start(bf16[32,4,8,128]{3,0,2,1:T(8,128)(2,1)S(1)} %copy.169), channel_id=1, source_target_pairs={{0,4},{4,8},{8,12},{12,0},{1,5},{5,9},{9,13},{13,1},{2,6},{6,10},{... | collective-permute-start | bytes 786440 | tf_op jit(solution)/shard_map/while/body/eval_jaxpr/ppermute | solution.py:19
  137.6 11.0 %collective-permute-start.2 = (bf16[32,4,8]{0,2,1:T(8,128)(2,1)S(1)}, bf16[32,4,8]{0,2,1:T(8,128)(2,1)S(1)}, u32[]{:S(2)}, u32[]{:S(2)}) collective-permute-start(bf16[32,4,8]{0,2,1:T(8,128)(2,1)S(1)} %fusion.103), channel_id=1, source_target_pairs={{0,4},{4,8},{8,12},{12,0},{1,5},{5,9},{9,13},{13,1},{2,6},{6,10},{... | collective-permute-start | bytes 6152 | tf_op jit(solution)/shard_map/while/body/eval_jaxpr/ppermute | solution.py:19
  138.2 10.5 %collective-permute-start.3 = (bf16[32,4,8]{0,2,1:T(8,128)(2,1)S(1)}, bf16[32,4,8]{0,2,1:T(8,128)(2,1)S(1)}, u32[]{:S(2)}, u32[]{:S(2)}) collective-permute-start(bf16[32,4,8]{0,2,1:T(8,128)(2,1)S(1)} %get-tuple-element.302), channel_id=1, source_target_pairs={{0,4},{4,8},{8,12},{12,0},{1,5},{5,9},{9,13},{13,1},{2,6},{6,10},{... | collective-permute-start | bytes 6152 | tf_op jit(solution)/shard_map/while/body/eval_jaxpr/ppermute | solution.py:19
  159.0 54.9 %all-reduce.2.cloned.1.call-start = ((), (), s32[]{:S(2)}) async-start(), calls=%async_computation.3 | async-start | bytes 524288 | tf_op jit(solution)/shard_map/psum | solution.py:137
  191.0 97.5 %reduce-scatter.3.cloned.1.call-start = ((), (), s32[]{:S(2)}) async-start(), calls=%async_computation.4 | async-start | bytes 4128768 | tf_op jit(solution)/shard_map/reduce_scatter | solution.py:145
  191.2 22.6 %copy-start = (bf16[128,1024]{1,0:T(8,128)(2,1)S(1)}, bf16[128,1024]{1,0:T(8,128)(2,1)}, u32[]{:S(2)}) copy-start(bf16[128,1024]{1,0:T(8,128)(2,1)} %param.19) | copy-start | bytes 786436
  191.2 39.6 %copy-start.1 = (f32[1024]{0:T(1024)S(1)}, f32[1024]{0:T(1024)}, u32[]{:S(2)}) copy-start(f32[1024]{0:T(1024)} %param.20) | copy-start | bytes 12292
  246.1 69.8 %all-gather.8.cloned.1.call-start = ((), (), s32[]{:S(2)}) async-start(), calls=%async_computation.5 | async-start | bytes 2064384 | tf_op jit(solution)/shard_map/all_gather | solution.py:153
  290.4 45.3 %reduce-scatter.5.cloned.1.call-start = ((), (), s32[]{:S(2)}) async-start(), calls=%async_computation.6 | async-start | bytes 393216 | tf_op jit(solution)/shard_map/reduce_scatter | solution.py:157
Sparse Core Ops, SparseCore 0:
  159.1 26.1 all-gather.5
  191.1 22.6 all-reduce.1
  246.2 42.2 reduce-scatter.2
  290.6 25.2 all-gather.7
  324.5 11.1 reduce-scatter.4
where the time goes:
time: 345 us; the launch traced here: 344 us
  waiting for transfers between devices  132 us (38%)
  matrix products  71.1 us (21%)
  blocking collectives  50.8 us (15%)
  local copies, waits for them, and re-layouts  35.3 us (10%)
  starting transfers between devices  20.3 us (6%)
  other arithmetic  19.8 us (6%)
  between operations  14 us (4%)
    reduce_scatter x1, waiting for transfers between devices, on_device(): lax.psum_scatter(jnp.dot(normed, merged_weight, preferred_element_type=jn...  42.4 us
    all_gather x1, waiting for transfers between devices, on_device(): lax.all_gather(attention, 'ctx', axis=0, tiled=True)  26.3 us
    all_gather x1, waiting for transfers between devices, on_device(): lax.all_gather(activated, ('ctx', 'khalf'), axis=0, tiled=True)  25.4 us
    ppermute x16, waiting for transfers between devices, shifted(): lax.ppermute(value, axis, [(i, (i + by) % devices) for i in range(devices)])  24.8 us
    dot_general x5, matrix products, attend(): jnp.einsum('rkgn,nkd->rkgd', weights.astype(jnp.bfloat16), valued, prefer...  23.6 us
    unnamed x12, local copies, waits for them, and re-layouts  22.8 us
    ppermute x16, starting transfers between devices, shifted(): lax.ppermute(value, axis, [(i, (i + by) % devices) for i in range(devices)])  20 us
    dot_general x5, matrix products, attend(): jnp.einsum('rkgd,nkd->rkgn', query_block, keyed, preferred_element_type=j...  18.1 us
  transfers between devices with their start and end apart: 21, of which 13 were waited for; matrix products, arithmetic and copies ran while one was open for 6% of the time, Pallas kernels for 0%

commit v1 on v0

v1 whole, which is shorter than its diff:
```python
import functools

import jax
import jax.numpy as jnp
from jax import lax
from jax.experimental import pallas as pl
from jax.experimental.pallas import tpu as pltpu
from jax.sharding import PartitionSpec as P

HQ = 64
DH = 128
BLOCK = 128

NEG = -1e30
EPSILON = 1e-05
MESH = pl.DeviceIdType.MESH
VMEM_LIMIT = 56 * 1024 * 1024


def peers(axis):
    n = lax.axis_size(axis)
    me = lax.axis_index(axis)
    return n, me, [lax.rem(me + o, n) for o in range(1, n)], [
        lax.rem(me + n - o, n) for o in range(1, n)
    ]


def meet(devices):
    barrier = pltpu.get_barrier_semaphore()
    for device in devices:
        pl.semaphore_signal(barrier, inc=1, device_id=device, device_id_type=MESH)
    pl.semaphore_wait(barrier, len(devices))


def remote(src, dst, send, recv, device):
    return pltpu.make_async_remote_copy(
        src_ref=src, dst_ref=dst, send_sem=send, recv_sem=recv, device_id=device, device_id_type=MESH
    )


def vmem(count):
    return [pl.BlockSpec(memory_space=pltpu.VMEM)] * count


def params(collective_id):
    return pltpu.CompilerParams(
        collective_id=collective_id, has_side_effects=True, vmem_limit_bytes=VMEM_LIMIT
    )


def gather_queries_kernel(q_ref, o_ref, zs, zr, ks, kr, own):
    n, me, after, before = peers("ctx")
    k = lax.axis_index("khalf")
    sibling = {"khalf": 1 - k}
    meet([{"ctx": c} for c in after] + [sibling])
    half = q_ref.shape[0] // 2
    mine = pl.ds(k * half, half)
    other = pl.ds((1 - k) * half, half)
    out = [
        remote(q_ref.at[mine], o_ref.at[me, mine], zs.at[i], zr.at[i], {"ctx": c})
        for i, c in enumerate(after)
    ]
    for copy in out:
        copy.start()
    local = pltpu.make_async_copy(q_ref, o_ref.at[me], own)
    local.start()
    on = []
    for i, c in enumerate(before):
        remote(o_ref.at[c, mine], o_ref.at[c, mine], zs.at[i], zr.at[i], sibling).wait_recv()
        copy = remote(o_ref.at[c, mine], o_ref.at[c, mine], ks.at[i], kr.at[i], sibling)
        copy.start()
        on.append(copy)
    for i, c in enumerate(before):
        remote(o_ref.at[c, other], o_ref.at[c, other], ks.at[i], kr.at[i], sibling).wait_recv()
    local.wait()
    for copy in out + on:
        copy.wait_send()


def gather_queries(q):
    n = lax.axis_size("ctx")
    sems = pltpu.SemaphoreType.DMA((max(n - 1, 1),))
    return pl.pallas_call(
        gather_queries_kernel,
        out_shape=jax.ShapeDtypeStruct((n,) + q.shape, q.dtype),
        in_specs=vmem(1),
        out_specs=vmem(1)[0],
        scratch_shapes=[sems] * 4 + [pltpu.SemaphoreType.DMA],
        compiler_params=params(0),
        name="gather_queries",
    )(q)


def to_rows(block):
    shape = block.shape
    flat = (shape[0] * shape[1] * shape[2], shape[3])
    if shape[2] % 16 == 0:
        return block.reshape(flat)
    return block.astype(jnp.float32).reshape(flat).astype(block.dtype)


def attend_kernel(chunk, place_ref, q_ref, k_ref, v_ref, nk_ref, nv_ref, acc_ref, st_ref):
    ctx, heads, rows, width = q_ref.shape
    count = ctx * heads * rows
    q = to_rows(q_ref[...])
    scale = width ** (-0.5)
    cached = place_ref[0]
    new_start = place_ref[1]
    use_new = place_ref[2]
    keys = k_ref.shape[0]

    def scored(block, usable):
        s = lax.dot_general(block, q, (((1,), (1,)), ((), ())), preferred_element_type=jnp.float32)
        s = jnp.where(usable, s * scale, NEG)
        return s

    def update(state, s, usable, values):
        m, l, acc = state
        m_new = jnp.maximum(m, jnp.max(s, axis=0, keepdims=True))
        p = jnp.where(usable, jnp.exp(s - m_new), 0.0)
        alpha = jnp.exp(m - m_new)
        l = l * alpha + jnp.sum(p, axis=0, keepdims=True)
        pv = lax.dot_general(
            values, p.astype(jnp.bfloat16), (((0,), (0,)), ((), ())), preferred_element_type=jnp.float32
        )
        return m_new, l, acc * alpha + pv

    state = (
        jnp.full((1, count), NEG, jnp.float32),
        jnp.zeros((1, count), jnp.float32),
        jnp.zeros((width, count), jnp.float32),
    )
    for start in range(0, keys, chunk):
        usable = lax.broadcasted_iota(jnp.int32, (chunk, 1), 0) + start < cached
        s = scored(k_ref[start : start + chunk, :], usable)
        state = update(state, s, usable, v_ref[start : start + chunk, :])
    new_count = nk_ref.shape[0]
    lane = lax.broadcasted_iota(jnp.int32, (1, count), 1)
    token = lane // (heads * rows) * rows + lane % rows
    key_at = lax.broadcasted_iota(jnp.int32, (new_count, 1), 0) + new_start
    usable = (key_at <= token) & (use_new > 0)
    s = scored(nk_ref[...], usable)
    m, l, acc = update(state, s, usable, nv_ref[...])
    acc_ref[...] = acc[None]
    st_ref[...] = jnp.zeros(st_ref.shape, jnp.float32)
    st_ref[0, 0:1, :] = m
    st_ref[0, 1:2, :] = l


def attend(q_all, keys, values, new_keys, new_values, place):
    ctx, heads, rows, width = q_all.shape
    groups = keys.shape[1] // width
    size = heads // groups
    count = ctx * size * rows
    length = keys.shape[0]
    chunk = next(c for c in (512, 256, 128, length) if length % c == 0)
    column = lambda n: pl.BlockSpec((n, width), lambda g: (0, g))
    return pl.pallas_call(
        functools.partial(attend_kernel, chunk),
        grid=(groups,),
        out_shape=(
            jax.ShapeDtypeStruct((groups, width, count), jnp.float32),
            jax.ShapeDtypeStruct((groups, 8, count), jnp.float32),
        ),
        in_specs=[
            pl.BlockSpec(memory_space=pltpu.SMEM),
            pl.BlockSpec((ctx, size, rows, width), lambda g: (0, g, 0, 0)),
            column(length),
            column(length),
            column(new_keys.shape[0]),
            column(new_keys.shape[0]),
        ],
        out_specs=(
            pl.BlockSpec((1, width, count), lambda g: (g, 0, 0)),
            pl.BlockSpec((1, 8, count), lambda g: (g, 0, 0)),
        ),
        compiler_params=pltpu.CompilerParams(vmem_limit_bytes=VMEM_LIMIT),
        name="attend",
    )(place, q_all, keys, values, new_keys, new_values)


def merge_kernel(
    acc_ref, st_ref, o_ref,
    sib_st, chip_st, ctx_st, part, sib_part, mine_part, ctx_part,
    s_st, r_st, s_z, r_z, s_p, r_p, s_a, r_a, s_g, r_g, s_k, r_k,
):
    n, me, after, before = peers("ctx")
    k = lax.axis_index("khalf")
    sibling = {"khalf": 1 - k}
    meet([{"ctx": c} for c in after] + [sibling])
    groups, width, count = acc_ref.shape
    _, heads, rows, _ = part.shape
    size = heads // groups
    half = heads // 2

    def stat_of(ref, at=()):
        return ref[at + (slice(None), slice(0, 1))], ref[at + (slice(None), slice(1, 2))]

    def joined(a, b):
        m = jnp.maximum(a[0], b[0])
        return m, a[1] * jnp.exp(a[0] - m) + b[1] * jnp.exp(b[0] - m)

    copy = remote(st_ref, sib_st, s_st, r_st, sibling)
    copy.start()
    copy.wait()
    own = stat_of(st_ref)
    chip = joined(own, stat_of(sib_st))
    chip_st[...] = jnp.zeros(chip_st.shape, jnp.float32)
    chip_st[:, 0:1, :] = chip[0]
    chip_st[:, 1:2, :] = chip[1]
    copies = [
        remote(chip_st, ctx_st.at[i], s_z.at[i], r_z.at[i], {"ctx": c}) for i, c in enumerate(after)
    ]
    for copy in copies:
        copy.start()
    total = chip
    for i, copy in enumerate(copies):
        copy.wait()
        total = joined(total, stat_of(ctx_st, (i,)))
    factor = jnp.exp(own[0] - total[0]) / total[1]
    for g in range(groups):
        scaled = jnp.transpose(acc_ref[g] * factor[g])
        part[:, g * size : (g + 1) * size] = scaled.reshape(n, size, rows, width).astype(part.dtype)
    copy = remote(part.at[:, pl.ds((1 - k) * half, half)], sib_part, s_p, r_p, sibling)
    copy.start()
    copy.wait()
    for c in range(n):
        mine_part[c] = (
            part[c, pl.ds(k * half, half)].astype(jnp.float32) + sib_part[c].astype(jnp.float32)
        ).astype(part.dtype)
    copies = [
        remote(mine_part.at[c], ctx_part.at[i], s_a.at[i], r_a.at[i], {"ctx": c})
        for i, c in enumerate(after)
    ]
    for copy in copies:
        copy.start()
    summed = mine_part[me].astype(jnp.float32)
    for i, copy in enumerate(copies):
        copy.wait()
        summed = summed + ctx_part[i].astype(jnp.float32)
    mine = pl.ds(k * half, half)
    other = pl.ds((1 - k) * half, half)
    o_ref[me, mine] = summed.astype(o_ref.dtype)
    out = [
        remote(o_ref.at[me, mine], o_ref.at[me, mine], s_g.at[i], r_g.at[i], {"ctx": c})
        for i, c in enumerate(after)
    ]
    on = [remote(o_ref.at[me, mine], o_ref.at[me, mine], s_k.at[n - 1], r_k.at[n - 1], sibling)]
    for copy in out + on:
        copy.start()
    for i, c in enumerate(before):
        remote(o_ref.at[c, mine], o_ref.at[c, mine], s_g.at[i], r_g.at[i], sibling).wait_recv()
        copy = remote(o_ref.at[c, mine], o_ref.at[c, mine], s_k.at[i], r_k.at[i], sibling)
        copy.start()
        on.append(copy)
    for i, c in enumerate(before + [me]):
        remote(o_ref.at[c, other], o_ref.at[c, other], s_k.at[i], r_k.at[i], sibling).wait_recv()
    for copy in out + on:
        copy.wait_send()


def merge(acc, stats, heads, rows):
    n = lax.axis_size("ctx")
    width = acc.shape[1]
    f32 = lambda *shape: pltpu.VMEM(shape, jnp.float32)
    b16 = lambda *shape: pltpu.VMEM(shape, jnp.bfloat16)
    one = pltpu.SemaphoreType.DMA
    many = pltpu.SemaphoreType.DMA((n,))
    return pl.pallas_call(
        merge_kernel,
        out_shape=jax.ShapeDtypeStruct((n, heads, rows, width), jnp.bfloat16),
        in_specs=vmem(2),
        out_specs=vmem(1)[0],
        scratch_shapes=[
            f32(*stats.shape), f32(*stats.shape), f32(max(n - 1, 1), *stats.shape),
            b16(n, heads, rows, width), b16(n, heads // 2, rows, width),
            b16(n, heads // 2, rows, width), b16(max(n - 1, 1), heads // 2, rows, width),
            one, one, many, many, one, one, many, many, many, many, many, many,
        ],
        compiler_params=params(1),
        name="merge",
    )(acc, stats)


def norm_kernel(
    total_width, p_ref, r_ref, g_ref, h_ref, n_ref, got, sq, sq_got, s_x, r_x, s_q, r_q
):
    n, me, after, _ = peers("ctx")
    k = lax.axis_index("khalf")
    _, _, across, _ = peers("kv")
    partners = [{"ctx": c} for c in after]
    partners += [{"ctx": c, "khalf": 1 - k} for c in [me] + after]
    meet([{"kv": c} for c in across] + partners)
    copies = [
        remote(p_ref, got.at[i], s_x.at[i], r_x.at[i], {"kv": c}) for i, c in enumerate(across)
    ]
    for copy in copies:
        copy.start()
    summed = p_ref[...].astype(jnp.float32)
    for i, copy in enumerate(copies):
        copy.wait()
        summed = summed + got[i].astype(jnp.float32)
    hidden = (r_ref[...].astype(jnp.float32) + summed).astype(h_ref.dtype)
    h_ref[...] = hidden
    values = hidden.astype(jnp.float32)
    squares = values * values
    rows, columns = values.shape
    lanes = squares[:, 0:128]
    for at in range(128, columns, 128):
        lanes = lanes + squares[:, at : at + 128]
    row = jnp.sum(jnp.transpose(lanes), axis=0, keepdims=True)
    sq[...] = jnp.broadcast_to(row, sq.shape)
    copies = [
        remote(sq, sq_got.at[i], s_q.at[i], r_q.at[i], device) for i, device in enumerate(partners)
    ]
    for copy in copies:
        copy.start()
    total = row
    for i, copy in enumerate(copies):
        copy.wait()
        total = total + sq_got[i, 0:1, :]
    factor = lax.rsqrt(total / total_width + EPSILON)
    column = jnp.transpose(jnp.broadcast_to(factor, (128, rows)))[:, 0:1]
    n_ref[...] = (values * column * g_ref[...]).astype(n_ref.dtype)


def norm(partial, residual, gain, total_width):
    rows, columns = partial.shape
    devices = lax.axis_size("ctx") * 2
    across = lax.axis_size("kv")
    shape = jax.ShapeDtypeStruct((rows, columns), jnp.bfloat16)
    many = lambda n: pltpu.SemaphoreType.DMA((max(n, 1),))
    return pl.pallas_call(
        functools.partial(norm_kernel, total_width),
        out_shape=(shape, shape),
        in_specs=vmem(3),
        out_specs=tuple(vmem(2)),
        scratch_shapes=[
            pltpu.VMEM((max(across - 1, 1), rows, columns), jnp.bfloat16),
            pltpu.VMEM((8, rows), jnp.float32),
            pltpu.VMEM((devices - 1, 8, rows), jnp.float32),
            many(across - 1), many(across - 1), many(devices - 1), many(devices - 1),
        ],
        compiler_params=params(2),
        name="norm",
    )(partial, residual, gain)


def finish_kernel(p_ref, h_ref, o_ref, got, s_x, r_x):
    n, me, across, _ = peers("kv")
    meet([{"kv": c} for c in across])
    copies = [
        remote(p_ref.at[c], got.at[i], s_x.at[i], r_x.at[i], {"kv": c}) for i, c in enumerate(across)
    ]
    for copy in copies:
        copy.start()
    summed = p_ref[me].astype(jnp.float32)
    for i, copy in enumerate(copies):
        copy.wait()
        summed = summed + got[i].astype(jnp.float32)
    o_ref[...] = (h_ref[me].astype(jnp.float32) + summed).astype(o_ref.dtype)


def finish(partial, hidden):
    n = lax.axis_size("kv")
    rows, columns = partial.shape
    block = (n, rows // n, columns)
    many = pltpu.SemaphoreType.DMA((max(n - 1, 1),))
    return pl.pallas_call(
        finish_kernel,
        out_shape=jax.ShapeDtypeStruct(block[1:], jnp.bfloat16),
        in_specs=vmem(2),
        out_specs=vmem(1)[0],
        scratch_shapes=[pltpu.VMEM((max(n - 1, 1),) + block[1:], jnp.bfloat16), many, many],
        compiler_params=params(3),
        name="finish",
    )(partial.reshape(block), hidden.reshape(block))


def on_device(
    queries,
    cache_keys,
    cache_values,
    new_keys,
    new_values,
    cache_blocks,
    residual,
    norm_gain,
    out_weight,
    gate_up,
    down_weight,
):
    rows = queries.shape[0]
    heads = queries.shape[1] // DH
    ctx = lax.axis_index("ctx")
    khalf = lax.axis_index("khalf")
    length = cache_keys.shape[0]
    start = (ctx * lax.axis_size("khalf") + khalf) * length
    place = jnp.stack(
        [cache_blocks[0] * BLOCK - start, ctx * rows, jnp.where(khalf == 0, 1, 0)]
    ).astype(jnp.int32)
    local_queries = queries.reshape(rows, heads, DH).transpose(1, 0, 2)
    q_all = gather_queries(local_queries)
    acc, stats = attend(q_all, cache_keys, cache_values, new_keys, new_values, place)
    attention = merge(acc, stats, heads, rows)
    tokens = attention.shape[0] * rows
    attention = attention.transpose(0, 2, 1, 3).reshape(tokens, heads * DH)
    partial_rows = jnp.dot(attention, out_weight, preferred_element_type=jnp.float32)
    total_width = out_weight.shape[1] * lax.axis_size("ctx") * lax.axis_size("khalf")
    hidden_state, normed = norm(
        partial_rows.astype(jnp.bfloat16), residual, norm_gain[None, :], total_width
    )
    both = jnp.einsum("tk,ksn->tsn", normed, gate_up, preferred_element_type=jnp.float32)
    both = lax.psum_scatter(
        both.astype(jnp.bfloat16), ("ctx", "khalf"), scatter_dimension=0, tiled=True
    ).astype(jnp.float32)
    activated = (jax.nn.silu(both[:, 0]) * both[:, 1]).astype(jnp.bfloat16)
    partial_out = jnp.dot(
        lax.all_gather(activated, ("ctx", "khalf"), axis=0, tiled=True),
        down_weight,
        preferred_element_type=jnp.float32,
    )
    return finish(partial_out.astype(jnp.bfloat16), hidden_state)


def solution(mesh):
    in_specs = (
        P(("groups", "ctx"), "kv"),
        P(("groups", "ctx", "khalf"), "kv"),
        P(("groups", "ctx", "khalf"), "kv"),
        P(("groups", "ctx"), "kv"),
        P(("groups", "ctx"), "kv"),
        P("groups"),
        P("groups", ("ctx", "khalf")),
        P(("ctx", "khalf")),
        P("kv", ("ctx", "khalf")),
        P(("ctx", "khalf"), None, "kv"),
        P("kv", ("ctx", "khalf")),
    )
    out_specs = P(("groups", "kv"), ("ctx", "khalf"))
    return jax.shard_map(
        on_device, mesh=mesh, in_specs=in_specs, out_specs=out_specs, check_vma=False
    )
```

time: 345 us -> 244 us (0.71)
  Pallas kernels: 0 us -> 118 us
  waiting for transfers between devices: 132 us -> 70.7 us
  blocking collectives: 50.8 us -> 0 us
  matrix products: 71.1 us -> 33.8 us
  local copies, waits for them, and re-layouts: 35.3 us -> 4.22 us
  starting transfers between devices: 20.3 us -> 0.04 us
  other arithmetic: 19.8 us -> 2.48 us
    pallas_call x0 -> x5, Pallas kernels: none -> 118 us  [the longest x1 47.4 us: merge(): pl.pallas_call(merge_kernel, out_shape=jax.ShapeDtypeStruct((n, heads, ro...]
    dot_general x12 -> x2, matrix products: 62.6 us -> 25.3 us  [the longest x1 19.6 us: on_device(): jnp.einsum('tk,ksn->tsn', normed, gate_up, preferred_element_type=jnp.flo...]
    all_gather x5 -> x0, blocking collectives: 34.9 us -> none  [the longest x1 15.3 us: on_device(): piece_keys = lax.all_gather(new_keys, 'ctx', axis=0, tiled=True)]
    all_gather x1 -> x0, waiting for transfers between devices: 26.3 us -> none  [on_device(): lax.all_gather(attention, 'ctx', axis=0, tiled=True)]
    ppermute x16 -> x0, waiting for transfers between devices: 24.8 us -> none  [shifted(): lax.ppermute(value, axis, [(i, (i + by) % devices) for i in range(devices)])]
    unnamed x12 -> x5, local copies, waits for them, and re-layouts: 22.8 us -> 1.84 us
    ppermute x16 -> x0, starting transfers between devices: 20 us -> none  [shifted(): lax.ppermute(value, axis, [(i, (i + by) % devices) for i in range(devices)])]
    psum x1 -> x0, blocking collectives: 15.9 us -> none  [normalize(): squares = lax.psum(jnp.sum(values32 * values32, axis=1), ('ctx', 'khalf'))]
  transfers between devices with their start and end apart: 21 -> 2, of which waited for: 13 -> 2; matrix products, arithmetic and copies ran while one was open for 6% -> 0% of each run, Pallas kernels for 0% -> 0%
where the time goes in v1:
time: 244 us; the launch traced here: 243 us
  Pallas kernels  118 us (48%)
  waiting for transfers between devices  70.7 us (29%)
  matrix products  33.8 us (14%)
  between operations  14.2 us (6%)
  local copies, waits for them, and re-layouts  4.22 us (2%)
  other arithmetic  2.48 us (1%)
    pallas_call x1, Pallas kernels, merge(): pl.pallas_call(merge_kernel, out_shape=jax.ShapeDtypeStruct((n, heads, ro...  47.4 us
    reduce_scatter x1, waiting for transfers between devices, on_device(): lax.psum_scatter(both.astype(jnp.bfloat16), ('ctx', 'khalf'), scatter_dim...  45.2 us
    pallas_call x1, Pallas kernels, attend(): pl.pallas_call(functools.partial(attend_kernel, chunk), grid=(groups,), o...  28.3 us
    all_gather x1, waiting for transfers between devices, on_device(): lax.all_gather(activated, ('ctx', 'khalf'), axis=0, tiled=True)  25.4 us
    dot_general x1, matrix products, on_device(): jnp.einsum('tk,ksn->tsn', normed, gate_up, preferred_element_type=jnp.flo...  19.6 us
    pallas_call x1, Pallas kernels, gather_queries(): pl.pallas_call(gather_queries_kernel, out_shape=jax.ShapeDtypeStruct((n,)...  18.2 us
    pallas_call x1, Pallas kernels, norm(): pl.pallas_call(functools.partial(norm_kernel, total_width), out_shape=(sh...  16.7 us
    dot_general x1, matrix products, on_device(): jnp.dot(lax.all_gather(activated, ('ctx', 'khalf'), axis=0, tiled=True),...  8.5 us
  transfers between devices with their start and end apart: 2, of which 2 were waited for; matrix products, arithmetic and copies ran while one was open for 0% of the time, Pallas kernels for 0%

profile of v1, /device:TPU:0, one launch (start us, length us, event | category | flops | bytes accessed | tf_op | source)
XLA Modules:
  0.0 243.4 jit_solution(11655161024451080445)
XLA Ops:
  6.5 0.0 copy-start
  6.5 0.0 reduce-scatter.2.cloned.1.call-start
  7.2 0.3 copy-done
  7.5 0.7 bitcast_bitcast_fusion.q_ref
  8.2 18.2 %gather_queries.1.q_ref = bf16[4,32,32,128]{3,2,1,0:T(8,128)(2,1)} custom-call(bf16[32,32,128]{2,1,0:T(8,128)(2,1)} %bitcast_bitcast_fusion.q_ref), custom_call_target="tpu_custom_call" | custom-call | tf_op jit(solution)/shard_map/gather_queries/pallas_call | solution.py:83
  26.5 0.6 pad_add_fusion.place_ref
  27.1 28.3 %attend.1 = (f32[4,128,1024]{2,1,0:T(8,128)}, f32[4,8,1024]{2,1,0:T(8,128)}) custom-call(s32[3]{0:T(128)} %pad_add_fusion.place_ref, bf16[4,32,32,128]{3,2,1,0:T(8,128)(2,1)} %gather_queries.1.q_ref, bf16[3072,512]{1,0:T(8,128)(2,1)} %k_ref.1, bf16[3072,512]{1,0:T(8,128)(2,1)} %v_ref.1, bf16[32,512]{1,0:T(8,128)(2,1)} %nk_ref.1, bf16[32,512]{1,0:T(8,128)(2,1)} %nv_ref.1), custom_call_target="tpu_custom_call" | custom-call | tf_op jit(solution)/shard_map/attend/pallas_call | solution.py:158
  55.3 47.4 %merge.1 = bf16[4,32,32,128]{3,2,1,0:T(8,128)(2,1)} custom-call(f32[4,128,1024]{2,1,0:T(8,128)} %get-tuple-element.9.acc_ref, f32[4,8,1024]{2,1,0:T(8,128)} %get-tuple-element.10.st_ref), custom_call_target="tpu_custom_call" | custom-call | tf_op jit(solution)/shard_map/merge/pallas_call | solution.py:269
  102.8 1.6 copy.14
  104.4 5.7 %convolution_convert_fusion.p_ref = bf16[128,1024]{1,0:T(8,128)(2,1)} fusion(bf16[4096,1024]{1,0:T(8,128)(2,1)} %param.19, bf16[16,8,32,128]{3,2,1,0:T(8,128)(2,1)S(1)} %bitcast.36), kind=kOutput, calls=%fused_computation.3 | convolution fusion | flops 1073872896 | bytes 9699328 | tf_op jit(solution)/shard_map/dot_general | solution.py:408
  110.1 16.7 %norm.1 = (bf16[128,1024]{1,0:T(8,128)(2,1)}, bf16[128,1024]{1,0:T(8,128)(2,1)}) custom-call(bf16[128,1024]{1,0:T(8,128)(2,1)} %convolution_convert_fusion.p_ref, bf16[128,1024]{1,0:T(8,128)(2,1)} %r_ref.1, f32[1,1024]{1,0:T(1,128)} %bitcast.40), custom_call_target="tpu_custom_call" | custom-call | tf_op jit(solution)/shard_map/norm/pallas_call | solution.py:333
  126.9 19.6 %fusion.2 = bf16[128,2,7168]{2,0,1:T(8,128)(2,1)} fusion(bf16[1024,2,7168]{2,1,0:T(2,128)(2,1)} %param.20, bf16[128,1024]{1,0:T(8,128)(2,1)} %get-tuple-element.11), kind=kOutput, calls=%fused_computation.2 | convolution fusion | flops 3759931392 | bytes 33292288 | tf_op jit(solution)/shard_map/tk,ksn->tsn/dot_general | solution.py:413
  146.5 0.0 reduce-scatter.2.cloned.1.call-update
  146.5 0.0 all-gather.2.cloned.1.call-start
  146.6 45.2 %reduce-scatter.2.cloned.1.call-done = bf16[16,2,7168]{2,0,1:T(8,128)(2,1)} async-done(((bf16[128,2,7168]{2,0,1:T(8,128)(2,1)}), bf16[16,2,7168]{2,0,1:T(8,128)(2,1)}) %reduce-scatter.2.cloned.1.call-update) | async-done | bytes 458768 | tf_op jit(solution)/shard_map/reduce_scatter | solution.py:414
  191.8 1.1 convert_element_type.17
  192.8 0.8 fusion.8
  193.6 0.0 all-gather.2.cloned.1.call-update
  193.7 0.0 copy-start.1
  193.7 25.4 %all-gather.2.cloned.1.call-done = bf16[128,7168]{1,0:T(8,128)(2,1)} async-done(((bf16[16,7168]{1,0:T(8,128)(2,1)}), bf16[128,7168]{1,0:T(8,128)(2,1)}) %all-gather.2.cloned.1.call-update) | async-done | bytes 1835024 | tf_op jit(solution)/shard_map/all_gather | solution.py:419
  219.1 8.5 %convolution_convert_fusion.1 = bf16[128,1024]{1,0:T(8,128)(2,1)} fusion(bf16[128,7168]{1,0:T(8,128)(2,1)} %all-gather.2.cloned.1.call-done, bf16[7168,1024]{1,0:T(8,128)(2,1)} %param.21), kind=kOutput, calls=%fused_computation.4 | convolution fusion | flops 1879179264 | bytes 16777216 | tf_op jit(solution)/shard_map/dot_general | solution.py:418
  227.6 7.4 %finish.1 = bf16[64,1024]{1,0:T(8,128)(2,1)} custom-call(bf16[2,64,1024]{2,1,0:T(8,128)(2,1)} %bitcast.38, bf16[2,64,1024]{2,1,0:T(8,128)(2,1)} %bitcast.39), custom_call_target="tpu_custom_call" | custom-call | tf_op jit(solution)/shard_map/finish/pallas_call | solution.py:369
  235.0 1.6 copy.29
  236.6 0.0 copy-done.1
Async XLA Ops:
  6.5 1.0 copy-start
  6.5 185.2 %reduce-scatter.2.cloned.1.call-start = ((), (), s32[]{:S(2)}) async-start(), calls=%async_computation.1 | async-start | bytes 4128768 | tf_op jit(solution)/shard_map/reduce_scatter | solution.py:414
  146.5 72.6 %all-gather.2.cloned.1.call-start = ((), (), s32[]{:S(2)}) async-start(), calls=%async_computation.2 | async-start | bytes 2064384 | tf_op jit(solution)/shard_map/all_gather | solution.py:419
  193.7 42.9 %copy-start.1 = (bf16[32,4096]{1,0:T(8,128)(2,1)S(1)}, bf16[32,4096]{1,0:T(8,128)(2,1)}, u32[]{:S(2)}) copy-start(bf16[32,4096]{1,0:T(8,128)(2,1)} %param.11) | copy-start | bytes 786436
Sparse Core Ops, SparseCore 0:
  146.6 45.0 reduce-scatter.1
  193.8 25.2 all-gather.1

commit v2 on v1

--- a/solution.py
+++ b/solution.py
@@ -346,35 +346,209 @@
     )(partial, residual, gain)
 
 
-def finish_kernel(p_ref, h_ref, o_ref, got, s_x, r_x):
-    n, me, across, _ = peers("kv")
-    meet([{"kv": c} for c in across])
+def ffn_kernel(
+    steps, x_ref, w_hbm, dn_hbm, h_ref, o_ref,
+    x2, wbuf, dbuf, own, sib_out, sib_in, rs_in, rs_out, act, part, psend, got,
+    w_sem, d_sem, s_s, s_r, r_s, r_r, a_s, a_r, f_s, f_r, x_s, x_r,
+):
+    n = lax.axis_size("ctx")
+    c = lax.axis_index("ctx")
+    k = lax.axis_index("khalf")
+    _, kv, across, _ = peers("kv")
+    sibling = {"khalf": 1 - k}
+    left, right = {"ctx": lax.rem(c + n - 1, n)}, {"ctx": lax.rem(c + 1, n)}
+    tokens, depth = x_ref.shape
+    half = w_hbm.shape[2] // 2
+    width = half // steps
+    toks = tokens // 2
+    w_rows = w_hbm.reshape(2 * depth, 2 * half)
+
+    def column(h, s):
+        return pl.multiple_of(h * half + s * width, 128)
+
+    def load(s, j):
+        h = k if j == 0 else 1 - k
+        slot = lax.rem(s, 2)
+        return pltpu.make_async_copy(
+            w_rows.at[:, pl.ds(column(h, s), width)], wbuf.at[slot, j], w_sem.at[slot, j]
+        )
+
+    for s in range(min(2, steps)):
+        load(s, 1).start()
+        load(s, 0).start()
+    down = pltpu.make_async_copy(dn_hbm, dbuf, d_sem)
+    down.start()
+    meet([left, right, sibling] + [{"kv": i} for i in across])
+
+    row = lax.broadcasted_iota(jnp.int32, (128, 256), 0)
+    lane = lax.broadcasted_iota(jnp.int32, (128, 256), 1)
+    for s in range(2):
+        spread = jnp.where(lane == 2 * row + s, 1.0, 0.0).astype(jnp.bfloat16)
+        for b in range(depth // 128):
+            x2[s * tokens : (s + 1) * tokens, b * 256 : (b + 1) * 256] = jnp.dot(
+                x_ref[:, b * 128 : (b + 1) * 128], spread, preferred_element_type=jnp.float32
+            ).astype(jnp.bfloat16)
+
+    def product(s, j):
+        load(s, j).wait()
+        both = jnp.dot(x2[...], wbuf[lax.rem(s, 2), j], preferred_element_type=jnp.float32)
+        return both.reshape(2, tokens, width)
+
+    def to_sibling(s):
+        return remote(sib_out.at[s], sib_in.at[s], s_s.at[s], s_r.at[s], sibling)
+
+    def toward(d):
+        return (left, right) if d == 0 else (right, left)
+
+    def sums(d, s):
+        return remote(rs_out.at[d, s], rs_in.at[d, s], r_s.at[d, s], r_r.at[d, s], toward(d)[0])
+
+    def region(d, h, s):
+        return act.at[pl.ds(d * toks, toks), pl.ds(column(h, s), width)]
+
+    def onward(d, s):
+        return remote(region(d, k, s), region(d, k, s), a_s.at[d, s], a_r.at[d, s], toward(d)[1])
+
+    def to_other(d, h, s):
+        return remote(region(d, h, s), region(d, h, s), f_s.at[d, s], f_r.at[d, s], sibling)
+
+    distance = (c, n - 1 - c)
+
+    def step(t, _):
+        @pl.when(t < steps)
+        def _():
+            sib_out[t] = product(t, 1).astype(jnp.bfloat16)
+            to_sibling(t).start()
+            own[t] = product(t, 0)
+
+            @pl.when(t + 2 < steps)
+            def _():
+                load(t + 2, 1).start()
+                load(t + 2, 0).start()
+
+        s = t - 1
+
+        @pl.when((s >= 0) & (s < steps))
+        def _():
+            to_sibling(s).wait_recv()
+            for d in range(2):
+                rows = slice(d * toks, (d + 1) * toks)
+
+                def total():
+                    return own[s, :, rows, :] + sib_in[s, :, rows, :].astype(jnp.float32)
+
+                @pl.when(distance[d] == n - 1)
+                def _():
+                    rs_out[d, s] = total().astype(jnp.bfloat16)
+                    sums(d, s).start()
+
+                @pl.when((distance[d] < n - 1) & (distance[d] > 0))
+                def _():
+                    sums(d, s).wait_recv()
+                    rs_out[d, s] = (total() + rs_in[d, s].astype(jnp.float32)).astype(jnp.bfloat16)
+                    sums(d, s).start()
+
+                @pl.when(distance[d] == 0)
+                def _():
+                    sums(d, s).wait_recv()
+                    both = total() + rs_in[d, s].astype(jnp.float32)
+                    gate = both[0]
+                    value = gate / (1.0 + jnp.exp(-gate)) * both[1]
+                    act[rows, pl.ds(column(k, s), width)] = value.astype(jnp.bfloat16)
+                    onward(d, s).start()
+                    to_other(d, k, s).start()
+
+        for d in range(2):
+            at = t - 2 * distance[d] - 2
+
+            @pl.when((distance[d] > 0) & (at >= 0) & (at < steps))
+            def _():
+                onward(d, at).wait_recv()
+
+                @pl.when(distance[d] < n - 1)
+                def _():
+                    onward(d, at).start()
+
+                to_other(d, k, at).start()
+
+        return 0
+
+    lax.fori_loop(0, steps + 2 * n, step, 0)
+
+    def settle(s, _):
+        to_sibling(s).wait_send()
+        for d in range(2):
+            to_other(d, 1 - k, s).wait_recv()
+            to_other(d, k, s).wait_send()
+
+            @pl.when(distance[d] > 0)
+            def _():
+                sums(d, s).wait_send()
+
+            @pl.when(distance[d] < n - 1)
+            def _():
+                onward(d, s).wait_send()
+
+        return 0
+
+    lax.fori_loop(0, steps, settle, 0)
+    down.wait()
+    part[...] = jnp.zeros(part.shape, jnp.float32)
+    deep = 2 * half // 7 if (2 * half) % (7 * 128) == 0 else 2 * half
+
+    def add(i, _):
+        at = pl.multiple_of(i * deep, 128)
+        part[...] += jnp.dot(
+            act[:, pl.ds(at, deep)], dbuf[pl.ds(at, deep), :], preferred_element_type=jnp.float32
+        )
+        return 0
+
+    lax.fori_loop(0, 2 * half // deep, add, 0)
+    rows = o_ref.shape[0]
+    for b in range(tokens // rows):
+        psend[b] = part[b * rows : (b + 1) * rows].astype(jnp.bfloat16)
     copies = [
-        remote(p_ref.at[c], got.at[i], s_x.at[i], r_x.at[i], {"kv": c}) for i, c in enumerate(across)
+        remote(psend.at[i], got.at[j], x_s.at[j], x_r.at[j], {"kv": i}) for j, i in enumerate(across)
     ]
     for copy in copies:
         copy.start()
-    summed = p_ref[me].astype(jnp.float32)
-    for i, copy in enumerate(copies):
+    summed = psend[kv].astype(jnp.float32)
+    for j, copy in enumerate(copies):
         copy.wait()
-        summed = summed + got[i].astype(jnp.float32)
-    o_ref[...] = (h_ref[me].astype(jnp.float32) + summed).astype(o_ref.dtype)
-
-
-def finish(partial, hidden):
+        summed = summed + got[j].astype(jnp.float32)
+    o_ref[...] = (h_ref[kv].astype(jnp.float32) + summed).astype(o_ref.dtype)
+
+
+def feed_forward(normed, gate_up, down_weight, hidden):
+    tokens, depth = normed.shape
+    half = gate_up.shape[2] // 2
+    steps = next(s for s in (7, 8, 4, 2, 1) if half % (s * 128) == 0)
+    width = half // steps
+    columns = down_weight.shape[1]
     n = lax.axis_size("kv")
-    rows, columns = partial.shape
-    block = (n, rows // n, columns)
-    many = pltpu.SemaphoreType.DMA((max(n - 1, 1),))
+    rows = tokens // n
+    b16 = lambda *shape: pltpu.VMEM(shape, jnp.bfloat16)
+    f32 = lambda *shape: pltpu.VMEM(shape, jnp.float32)
+    many = lambda *shape: pltpu.SemaphoreType.DMA(shape)
+    anywhere = pl.BlockSpec(memory_space=pl.ANY)
     return pl.pallas_call(
-        finish_kernel,
-        out_shape=jax.ShapeDtypeStruct(block[1:], jnp.bfloat16),
-        in_specs=vmem(2),
+        functools.partial(ffn_kernel, steps),
+        out_shape=jax.ShapeDtypeStruct((rows, columns), jnp.bfloat16),
+        in_specs=[vmem(1)[0], anywhere, anywhere, vmem(1)[0]],
         out_specs=vmem(1)[0],
-        scratch_shapes=[pltpu.VMEM((max(n - 1, 1),) + block[1:], jnp.bfloat16), many, many],
+        scratch_shapes=[
+            b16(2 * tokens, 2 * depth), b16(2, 2, 2 * depth, width), b16(2 * half, columns),
+            f32(steps, 2, tokens, width), b16(steps, 2, tokens, width), b16(steps, 2, tokens, width),
+            b16(2, steps, 2, tokens // 2, width), b16(2, steps, 2, tokens // 2, width),
+            b16(tokens, 2 * half), f32(tokens, columns), b16(n, rows, columns),
+            b16(max(n - 1, 1), rows, columns),
+            many(2, 2), many(), many(steps), many(steps), many(2, steps), many(2, steps),
+            many(2, steps), many(2, steps), many(2, steps), many(2, steps),
+            many(max(n - 1, 1)), many(max(n - 1, 1)),
+        ],
         compiler_params=params(3),
-        name="finish",
-    )(partial.reshape(block), hidden.reshape(block))
+        name="feed_forward",
+    )(normed, gate_up, down_weight, hidden.reshape(n, rows, columns))
 
 
 def on_device(
@@ -410,17 +584,7 @@
     hidden_state, normed = norm(
         partial_rows.astype(jnp.bfloat16), residual, norm_gain[None, :], total_width
     )
-    both = jnp.einsum("tk,ksn->tsn", normed, gate_up, preferred_element_type=jnp.float32)
-    both = lax.psum_scatter(
-        both.astype(jnp.bfloat16), ("ctx", "khalf"), scatter_dimension=0, tiled=True
-    ).astype(jnp.float32)
-    activated = (jax.nn.silu(both[:, 0]) * both[:, 1]).astype(jnp.bfloat16)
-    partial_out = jnp.dot(
-        lax.all_gather(activated, ("ctx", "khalf"), axis=0, tiled=True),
-        down_weight,
-        preferred_element_type=jnp.float32,
-    )
-    return finish(partial_out.astype(jnp.bfloat16), hidden_state)
+    return feed_forward(normed, gate_up, down_weight, hidden_state)
 
 
 def solution(mesh):

time: 244 us -> 338 us (1.39)
  Pallas kernels: 118 us -> 327 us
  waiting for transfers between devices: 70.7 us -> 0 us
  matrix products: 33.8 us -> 5.71 us
  between operations: 14.2 us -> 0.73 us
    pallas_call x1, Pallas kernels: 7.38 us -> 216 us  [feed_forward(): pl.pallas_call(functools.partial(ffn_kernel, steps), out_shape=jax.ShapeD...]
    reduce_scatter x1 -> x0, waiting for transfers between devices: 45.2 us -> none  [on_device(): lax.psum_scatter(both.astype(jnp.bfloat16), ('ctx', 'khalf'), scatter_dim...]
    dot_general x2 -> x0, matrix products: 28.1 us -> none  [the longest x1 19.6 us: on_device(): jnp.einsum('tk,ksn->tsn', normed, gate_up, preferred_element_type=jnp.flo...]
    all_gather x1 -> x0, waiting for transfers between devices: 25.4 us -> none  [on_device(): lax.all_gather(activated, ('ctx', 'khalf'), axis=0, tiled=True)]
  transfers between devices with their start and end apart: 2 -> 0, of which waited for: 2 -> 0; matrix products, arithmetic and copies ran while one was open for 0% -> 0% of each run, Pallas kernels for 0% -> 0%
where the time goes in v2:
time: 338 us
  Pallas kernels  327 us (97%)
  matrix products  5.71 us (2%)
  local copies, waits for them, and re-layouts  3.94 us (1%)
    pallas_call x1, Pallas kernels, feed_forward(): pl.pallas_call(functools.partial(ffn_kernel, steps), out_shape=jax.ShapeD...  216 us
    pallas_call x1, Pallas kernels, merge(): pl.pallas_call(merge_kernel, out_shape=jax.ShapeDtypeStruct((n, heads, ro...  47.4 us
    pallas_call x1, Pallas kernels, attend(): pl.pallas_call(functools.partial(attend_kernel, chunk), grid=(groups,), o...  28.3 us
    pallas_call x1, Pallas kernels, gather_queries(): pl.pallas_call(gather_queries_kernel, out_shape=jax.ShapeDtypeStruct((n,)...  18.2 us
    pallas_call x1, Pallas kernels, norm(): pl.pallas_call(functools.partial(norm_kernel, total_width), out_shape=(sh...  16.8 us

profile of v2, /device:TPU:0, one launch (start us, length us, event | category | flops | bytes accessed | tf_op | source)
XLA Modules:
  0.0 338.0 jit_solution(3534962158095486420)
XLA Ops:
  0.0 0.0 copy-start
  0.7 0.6 pad_add_fusion.place_ref
  1.3 0.0 copy-done
  1.3 0.7 bitcast_bitcast_fusion.q_ref
  2.0 18.2 %gather_queries.1.q_ref = bf16[4,32,32,128]{3,2,1,0:T(8,128)(2,1)} custom-call(bf16[32,32,128]{2,1,0:T(8,128)(2,1)} %bitcast_bitcast_fusion.q_ref), custom_call_target="tpu_custom_call" | custom-call | tf_op jit(solution)/shard_map/gather_queries/pallas_call | solution.py:83
  20.3 28.3 %attend.1 = (f32[4,128,1024]{2,1,0:T(8,128)}, f32[4,8,1024]{2,1,0:T(8,128)}) custom-call(s32[3]{0:T(128)} %pad_add_fusion.place_ref, bf16[4,32,32,128]{3,2,1,0:T(8,128)(2,1)} %gather_queries.1.q_ref, bf16[3072,512]{1,0:T(8,128)(2,1)} %k_ref.1, bf16[3072,512]{1,0:T(8,128)(2,1)} %v_ref.1, bf16[32,512]{1,0:T(8,128)(2,1)} %nk_ref.1, bf16[32,512]{1,0:T(8,128)(2,1)} %nv_ref.1), custom_call_target="tpu_custom_call" | custom-call | tf_op jit(solution)/shard_map/attend/pallas_call | solution.py:158
  48.6 47.4 %merge.1 = bf16[4,32,32,128]{3,2,1,0:T(8,128)(2,1)} custom-call(f32[4,128,1024]{2,1,0:T(8,128)} %get-tuple-element.9.acc_ref, f32[4,8,1024]{2,1,0:T(8,128)} %get-tuple-element.10.st_ref), custom_call_target="tpu_custom_call" | custom-call | tf_op jit(solution)/shard_map/merge/pallas_call | solution.py:269
  96.0 1.6 copy.13
  97.6 5.7 %convolution_convert_fusion.p_ref = bf16[128,1024]{1,0:T(8,128)(2,1)} fusion(bf16[4096,1024]{1,0:T(8,128)(2,1)} %param.19, bf16[16,8,32,128]{3,2,1,0:T(8,128)(2,1)S(1)} %bitcast.20), kind=kOutput, calls=%fused_computation | convolution fusion | flops 1073872896 | bytes 9699328 | tf_op jit(solution)/shard_map/dot_general | solution.py:582
  103.3 16.8 %norm.1 = (bf16[128,1024]{1,0:T(8,128)(2,1)}, bf16[128,1024]{1,0:T(8,128)(2,1)}) custom-call(bf16[128,1024]{1,0:T(8,128)(2,1)} %convolution_convert_fusion.p_ref, bf16[128,1024]{1,0:T(8,128)(2,1)} %r_ref.1, f32[1,1024]{1,0:T(1,128)} %bitcast.23), custom_call_target="tpu_custom_call" | custom-call | tf_op jit(solution)/shard_map/norm/pallas_call | solution.py:333
  120.2 216.3 %feed_forward.1 = bf16[64,1024]{1,0:T(8,128)(2,1)} custom-call(bf16[128,1024]{1,0:T(8,128)(2,1)} %get-tuple-element.11.x_ref, bf16[1024,2,7168]{2,1,0:T(2,128)(2,1)} %w_hbm.1, bf16[7168,1024]{1,0:T(8,128)(2,1)} %dn_hbm.1, bf16[2,64,1024]{2,1,0:T(8,128)(2,1)} %bitcast.22), custom_call_target="tpu_custom_call" | custom-call | tf_op jit(solution)/shard_map/feed_forward/pallas_call | solution.py:534
  336.5 1.6 copy.23
Async XLA Ops:
  0.0 1.3 copy-start

commit v3 on v2

--- a/solution.py
+++ b/solution.py
@@ -48,44 +48,85 @@
     )
 
 
-def gather_queries_kernel(q_ref, o_ref, zs, zr, ks, kr, own):
-    n, me, after, before = peers("ctx")
+def gather_line(o_ref, with_own, zs, zr, ks, kr):
+    n, me, _, _ = peers("ctx")
     k = lax.axis_index("khalf")
     sibling = {"khalf": 1 - k}
-    meet([{"ctx": c} for c in after] + [sibling])
-    half = q_ref.shape[0] // 2
-    mine = pl.ds(k * half, half)
-    other = pl.ds((1 - k) * half, half)
-    out = [
-        remote(q_ref.at[mine], o_ref.at[me, mine], zs.at[i], zr.at[i], {"ctx": c})
-        for i, c in enumerate(after)
-    ]
-    for copy in out:
-        copy.start()
-    local = pltpu.make_async_copy(q_ref, o_ref.at[me], own)
-    local.start()
-    on = []
-    for i, c in enumerate(before):
-        remote(o_ref.at[c, mine], o_ref.at[c, mine], zs.at[i], zr.at[i], sibling).wait_recv()
-        copy = remote(o_ref.at[c, mine], o_ref.at[c, mine], ks.at[i], kr.at[i], sibling)
-        copy.start()
-        on.append(copy)
-    for i, c in enumerate(before):
-        remote(o_ref.at[c, other], o_ref.at[c, other], ks.at[i], kr.at[i], sibling).wait_recv()
-    local.wait()
-    for copy in out + on:
-        copy.wait_send()
+    beside = ({"ctx": lax.rem(me + 1, n)}, {"ctx": lax.rem(me + n - 1, n)})
+    has_next = (me < n - 1, me > 0)
+    half = o_ref.shape[1] // 2
+    mine, other = pl.ds(k * half, half), pl.ds((1 - k) * half, half)
+
+    def pass_on(b, d):
+        block = o_ref.at[b, mine]
+        return remote(block, block, zs.at[d, b], zr.at[b], beside[d])
+
+    def across(b, part):
+        block = o_ref.at[b, part]
+        return remote(block, block, ks.at[b], kr.at[b], sibling)
+
+    for d in range(2):
+
+        @pl.when(has_next[d])
+        def _():
+            pass_on(me, d).start()
+
+    if with_own:
+        across(me, mine).start()
+    for hop in range(1, n):
+        for d in range(2):
+            b = me - hop if d == 0 else me + hop
+
+            @pl.when((b >= 0) & (b < n))
+            def _():
+                pass_on(b, d).wait_recv()
+
+                @pl.when(has_next[d])
+                def _():
+                    pass_on(b, d).start()
+
+                across(b, mine).start()
+
+    for b in range(n):
+
+        @pl.when(jnp.logical_or(with_own, me != b))
+        def _():
+            across(b, other).wait_recv()
+            across(b, mine).wait_send()
+
+        for d in range(2):
+
+            @pl.when(has_next[d] & ((b <= me) if d == 0 else (b >= me)))
+            def _():
+                pass_on(b, d).wait_send()
+
+
+def gather_queries_kernel(q_ref, o_ref, zs, zr, ks, kr):
+    n, me, _, _ = peers("ctx")
+    meet(
+        [
+            {"ctx": lax.rem(me + 1, n)},
+            {"ctx": lax.rem(me + n - 1, n)},
+            {"khalf": 1 - lax.axis_index("khalf")},
+        ]
+    )
+    o_ref[me] = q_ref[...]
+    gather_line(o_ref, False, zs, zr, ks, kr)
+
+
+def line_sems(n):
+    sem = pltpu.SemaphoreType.DMA
+    return [sem((2, n)), sem((n,)), sem((n,)), sem((n,))]
 
 
 def gather_queries(q):
     n = lax.axis_size("ctx")
-    sems = pltpu.SemaphoreType.DMA((max(n - 1, 1),))
     return pl.pallas_call(
         gather_queries_kernel,
         out_shape=jax.ShapeDtypeStruct((n,) + q.shape, q.dtype),
         in_specs=vmem(1),
         out_specs=vmem(1)[0],
-        scratch_shapes=[sems] * 4 + [pltpu.SemaphoreType.DMA],
+        scratch_shapes=line_sems(n),
         compiler_params=params(0),
         name="gather_queries",
     )(q)
@@ -142,9 +183,9 @@
     s = scored(nk_ref[...], usable)
     m, l, acc = update(state, s, usable, nv_ref[...])
     acc_ref[...] = acc[None]
-    st_ref[...] = jnp.zeros(st_ref.shape, jnp.float32)
-    st_ref[0, 0:1, :] = m
-    st_ref[0, 1:2, :] = l
+    group = pl.program_id(0)
+    st_ref[pl.ds(group, 1), :] = m
+    st_ref[pl.ds(group + st_ref.shape[0] // 2, 1), :] = l
 
 
 def attend(q_all, keys, values, new_keys, new_values, place):
@@ -160,7 +201,7 @@
         grid=(groups,),
         out_shape=(
             jax.ShapeDtypeStruct((groups, width, count), jnp.float32),
-            jax.ShapeDtypeStruct((groups, 8, count), jnp.float32),
+            jax.ShapeDtypeStruct((2 * groups, count), jnp.float32),
         ),
         in_specs=[
             pl.BlockSpec(memory_space=pltpu.SMEM),
@@ -172,7 +213,7 @@
         ],
         out_specs=(
             pl.BlockSpec((1, width, count), lambda g: (g, 0, 0)),
-            pl.BlockSpec((1, 8, count), lambda g: (g, 0, 0)),
+            pl.BlockSpec((2 * groups, count), lambda g: (0, 0)),
         ),
         compiler_params=pltpu.CompilerParams(vmem_limit_bytes=VMEM_LIMIT),
         name="attend",
@@ -182,7 +223,7 @@
 def merge_kernel(
     acc_ref, st_ref, o_ref,
     sib_st, chip_st, ctx_st, part, sib_part, mine_part, ctx_part,
-    s_st, r_st, s_z, r_z, s_p, r_p, s_a, r_a, s_g, r_g, s_k, r_k,
+    s_st, r_st, s_z, r_z, s_p, r_p, s_a, r_a, zs, zr, ks, kr,
 ):
     n, me, after, before = peers("ctx")
     k = lax.axis_index("khalf")
@@ -194,7 +235,7 @@
     half = heads // 2
 
     def stat_of(ref, at=()):
-        return ref[at + (slice(None), slice(0, 1))], ref[at + (slice(None), slice(1, 2))]
+        return ref[at + (slice(0, groups),)], ref[at + (slice(groups, 2 * groups),)]
 
     def joined(a, b):
         m = jnp.maximum(a[0], b[0])
@@ -205,9 +246,8 @@
     copy.wait()
     own = stat_of(st_ref)
     chip = joined(own, stat_of(sib_st))
-    chip_st[...] = jnp.zeros(chip_st.shape, jnp.float32)
-    chip_st[:, 0:1, :] = chip[0]
-    chip_st[:, 1:2, :] = chip[1]
+    chip_st[0:groups] = chip[0]
+    chip_st[groups : 2 * groups] = chip[1]
     copies = [
         remote(chip_st, ctx_st.at[i], s_z.at[i], r_z.at[i], {"ctx": c}) for i, c in enumerate(after)
     ]
@@ -219,43 +259,31 @@
         total = joined(total, stat_of(ctx_st, (i,)))
     factor = jnp.exp(own[0] - total[0]) / total[1]
     for g in range(groups):
-        scaled = jnp.transpose(acc_ref[g] * factor[g])
+        scaled = jnp.transpose(acc_ref[g] * factor[g : g + 1])
         part[:, g * size : (g + 1) * size] = scaled.reshape(n, size, rows, width).astype(part.dtype)
-    copy = remote(part.at[:, pl.ds((1 - k) * half, half)], sib_part, s_p, r_p, sibling)
-    copy.start()
-    copy.wait()
-    for c in range(n):
-        mine_part[c] = (
-            part[c, pl.ds(k * half, half)].astype(jnp.float32) + sib_part[c].astype(jnp.float32)
-        ).astype(part.dtype)
-    copies = [
-        remote(mine_part.at[c], ctx_part.at[i], s_a.at[i], r_a.at[i], {"ctx": c})
-        for i, c in enumerate(after)
-    ]
-    for copy in copies:
-        copy.start()
-    summed = mine_part[me].astype(jnp.float32)
-    for i, copy in enumerate(copies):
-        copy.wait()
-        summed = summed + ctx_part[i].astype(jnp.float32)
     mine = pl.ds(k * half, half)
     other = pl.ds((1 - k) * half, half)
+    swaps = [
+        remote(part.at[c, other], sib_part.at[c], s_p.at[i], r_p.at[i], sibling)
+        for i, c in enumerate(after + [me])
+    ]
+    meet_sums = []
+    for copy in swaps:
+        copy.start()
+    for i, c in enumerate(after + [me]):
+        swaps[i].wait_recv()
+        summed = part[c, mine].astype(jnp.float32) + sib_part[c].astype(jnp.float32)
+        if i < n - 1:
+            mine_part[c] = summed.astype(part.dtype)
+            copy = remote(mine_part.at[c], ctx_part.at[i], s_a.at[i], r_a.at[i], {"ctx": c})
+            copy.start()
+            meet_sums.append(copy)
+    for i, copy in enumerate(meet_sums):
+        copy.wait_recv()
+        summed = summed + ctx_part[i].astype(jnp.float32)
     o_ref[me, mine] = summed.astype(o_ref.dtype)
-    out = [
-        remote(o_ref.at[me, mine], o_ref.at[me, mine], s_g.at[i], r_g.at[i], {"ctx": c})
-        for i, c in enumerate(after)
-    ]
-    on = [remote(o_ref.at[me, mine], o_ref.at[me, mine], s_k.at[n - 1], r_k.at[n - 1], sibling)]
-    for copy in out + on:
-        copy.start()
-    for i, c in enumerate(before):
-        remote(o_ref.at[c, mine], o_ref.at[c, mine], s_g.at[i], r_g.at[i], sibling).wait_recv()
-        copy = remote(o_ref.at[c, mine], o_ref.at[c, mine], s_k.at[i], r_k.at[i], sibling)
-        copy.start()
-        on.append(copy)
-    for i, c in enumerate(before + [me]):
-        remote(o_ref.at[c, other], o_ref.at[c, other], s_k.at[i], r_k.at[i], sibling).wait_recv()
-    for copy in out + on:
+    gather_line(o_ref, True, zs, zr, ks, kr)
+    for copy in swaps + meet_sums:
         copy.wait_send()
 
 
@@ -275,7 +303,7 @@
             f32(*stats.shape), f32(*stats.shape), f32(max(n - 1, 1), *stats.shape),
             b16(n, heads, rows, width), b16(n, heads // 2, rows, width),
             b16(n, heads // 2, rows, width), b16(max(n - 1, 1), heads // 2, rows, width),
-            one, one, many, many, one, one, many, many, many, many, many, many,
+            one, one, many, many, many, many, many, many, *line_sems(n),
         ],
         compiler_params=params(1),
         name="merge",
@@ -347,9 +375,9 @@
 
 
 def ffn_kernel(
-    steps, x_ref, w_hbm, dn_hbm, h_ref, o_ref,
-    x2, wbuf, dbuf, own, sib_out, sib_in, rs_in, rs_out, act, part, psend, got,
-    w_sem, d_sem, s_s, s_r, r_s, r_r, a_s, a_r, f_s, f_r, x_s, x_r,
+    steps, b_ref, dn_hbm, h_ref, o_ref,
+    dbuf, sib_in, rs_in, rs_out, act, part, psend, got,
+    d_sem, s_s, s_r, r_s, r_r, a_s, a_r, f_s, f_r, x_s, x_r,
 ):
     n = lax.axis_size("ctx")
     c = lax.axis_index("ctx")
@@ -357,45 +385,22 @@
     _, kv, across, _ = peers("kv")
     sibling = {"khalf": 1 - k}
     left, right = {"ctx": lax.rem(c + n - 1, n)}, {"ctx": lax.rem(c + 1, n)}
-    tokens, depth = x_ref.shape
-    half = w_hbm.shape[2] // 2
+    tokens = b_ref.shape[1]
+    half = b_ref.shape[2] // 2
     width = half // steps
     toks = tokens // 2
-    w_rows = w_hbm.reshape(2 * depth, 2 * half)
 
     def column(h, s):
         return pl.multiple_of(h * half + s * width, 128)
 
-    def load(s, j):
-        h = k if j == 0 else 1 - k
-        slot = lax.rem(s, 2)
-        return pltpu.make_async_copy(
-            w_rows.at[:, pl.ds(column(h, s), width)], wbuf.at[slot, j], w_sem.at[slot, j]
-        )
-
-    for s in range(min(2, steps)):
-        load(s, 1).start()
-        load(s, 0).start()
     down = pltpu.make_async_copy(dn_hbm, dbuf, d_sem)
     down.start()
     meet([left, right, sibling] + [{"kv": i} for i in across])
 
-    row = lax.broadcasted_iota(jnp.int32, (128, 256), 0)
-    lane = lax.broadcasted_iota(jnp.int32, (128, 256), 1)
-    for s in range(2):
-        spread = jnp.where(lane == 2 * row + s, 1.0, 0.0).astype(jnp.bfloat16)
-        for b in range(depth // 128):
-            x2[s * tokens : (s + 1) * tokens, b * 256 : (b + 1) * 256] = jnp.dot(
-                x_ref[:, b * 128 : (b + 1) * 128], spread, preferred_element_type=jnp.float32
-            ).astype(jnp.bfloat16)
-
-    def product(s, j):
-        load(s, j).wait()
-        both = jnp.dot(x2[...], wbuf[lax.rem(s, 2), j], preferred_element_type=jnp.float32)
-        return both.reshape(2, tokens, width)
-
     def to_sibling(s):
-        return remote(sib_out.at[s], sib_in.at[s], s_s.at[s], s_r.at[s], sibling)
+        return remote(
+            b_ref.at[:, :, pl.ds(column(1 - k, s), width)], sib_in.at[s], s_s.at[s], s_r.at[s], sibling
+        )
 
     def toward(d):
         return (left, right) if d == 0 else (right, left)
@@ -414,19 +419,11 @@
 
     distance = (c, n - 1 - c)
 
+    for s in range(steps):
+        to_sibling(s).start()
+
     def step(t, _):
-        @pl.when(t < steps)
-        def _():
-            sib_out[t] = product(t, 1).astype(jnp.bfloat16)
-            to_sibling(t).start()
-            own[t] = product(t, 0)
-
-            @pl.when(t + 2 < steps)
-            def _():
-                load(t + 2, 1).start()
-                load(t + 2, 0).start()
-
-        s = t - 1
+        s = t
 
         @pl.when((s >= 0) & (s < steps))
         def _():
@@ -435,7 +432,8 @@
                 rows = slice(d * toks, (d + 1) * toks)
 
                 def total():
-                    return own[s, :, rows, :] + sib_in[s, :, rows, :].astype(jnp.float32)
+                    own = b_ref[:, rows, pl.ds(column(k, s), width)].astype(jnp.float32)
+                    return own + sib_in[s, :, rows, :].astype(jnp.float32)
 
                 @pl.when(distance[d] == n - 1)
                 def _():
@@ -459,7 +457,7 @@
                     to_other(d, k, s).start()
 
         for d in range(2):
-            at = t - 2 * distance[d] - 2
+            at = t - 2 * distance[d] - 1
 
             @pl.when((distance[d] > 0) & (at >= 0) & (at < steps))
             def _():
@@ -519,9 +517,9 @@
     o_ref[...] = (h_ref[kv].astype(jnp.float32) + summed).astype(o_ref.dtype)
 
 
-def feed_forward(normed, gate_up, down_weight, hidden):
-    tokens, depth = normed.shape
-    half = gate_up.shape[2] // 2
+def feed_forward(both, down_weight, hidden):
+    _, tokens, local_hidden = both.shape
+    half = local_hidden // 2
     steps = next(s for s in (7, 8, 4, 2, 1) if half % (s * 128) == 0)
     width = half // steps
     columns = down_weight.shape[1]
@@ -534,21 +532,20 @@
     return pl.pallas_call(
         functools.partial(ffn_kernel, steps),
         out_shape=jax.ShapeDtypeStruct((rows, columns), jnp.bfloat16),
-        in_specs=[vmem(1)[0], anywhere, anywhere, vmem(1)[0]],
+        in_specs=[vmem(1)[0], anywhere, vmem(1)[0]],
         out_specs=vmem(1)[0],
         scratch_shapes=[
-            b16(2 * tokens, 2 * depth), b16(2, 2, 2 * depth, width), b16(2 * half, columns),
-            f32(steps, 2, tokens, width), b16(steps, 2, tokens, width), b16(steps, 2, tokens, width),
+            b16(2 * half, columns), b16(steps, 2, tokens, width),
             b16(2, steps, 2, tokens // 2, width), b16(2, steps, 2, tokens // 2, width),
             b16(tokens, 2 * half), f32(tokens, columns), b16(n, rows, columns),
             b16(max(n - 1, 1), rows, columns),
-            many(2, 2), many(), many(steps), many(steps), many(2, steps), many(2, steps),
+            many(), many(steps), many(steps), many(2, steps), many(2, steps),
             many(2, steps), many(2, steps), many(2, steps), many(2, steps),
             many(max(n - 1, 1)), many(max(n - 1, 1)),
         ],
         compiler_params=params(3),
         name="feed_forward",
-    )(normed, gate_up, down_weight, hidden.reshape(n, rows, columns))
+    )(both, down_weight, hidden.reshape(n, rows, columns))
 
 
 def on_device(
@@ -584,7 +581,8 @@
     hidden_state, normed = norm(
         partial_rows.astype(jnp.bfloat16), residual, norm_gain[None, :], total_width
     )
-    return feed_forward(normed, gate_up, down_weight, hidden_state)
+    both = jnp.einsum("tk,ksn->stn", normed, gate_up, preferred_element_type=jnp.float32)
+    return feed_forward(both.astype(jnp.bfloat16), down_weight, hidden_state)
 
 
 def solution(mesh):

time: 338 us -> 345 us (1.021)
  matrix products: 5.71 us -> 25.3 us
  Pallas kernels: 327 us -> 314 us
    dot_general x0 -> x1, matrix products: none -> 19.6 us  [on_device(): jnp.einsum('tk,ksn->stn', normed, gate_up, preferred_element_type=jnp.flo...]
    pallas_call x1, Pallas kernels: 47.4 us -> 39.9 us  [merge(): pl.pallas_call(merge_kernel, out_shape=jax.ShapeDtypeStruct((n, heads, ro...]
    pallas_call x1, Pallas kernels: 216 us -> 210 us  [feed_forward(): pl.pallas_call(functools.partial(ffn_kernel, steps), out_shape=jax.ShapeD...]
where the time goes in v3:
time: 345 us; the launch traced here: 344 us
  Pallas kernels  314 us (91%)
  matrix products  25.3 us (7%)
  local copies, waits for them, and re-layouts  3.95 us (1%)
    pallas_call x1, Pallas kernels, feed_forward(): pl.pallas_call(functools.partial(ffn_kernel, steps), out_shape=jax.ShapeD...  210 us
    pallas_call x1, Pallas kernels, merge(): pl.pallas_call(merge_kernel, out_shape=jax.ShapeDtypeStruct((n, heads, ro...  39.9 us
    pallas_call x1, Pallas kernels, attend(): pl.pallas_call(functools.partial(attend_kernel, chunk), grid=(groups,), o...  28.3 us
    pallas_call x1, Pallas kernels, gather_queries(): pl.pallas_call(gather_queries_kernel, out_shape=jax.ShapeDtypeStruct((n,)...  19.6 us
    dot_general x1, matrix products, on_device(): jnp.einsum('tk,ksn->stn', normed, gate_up, preferred_element_type=jnp.flo...  19.6 us
    pallas_call x1, Pallas kernels, norm(): pl.pallas_call(functools.partial(norm_kernel, total_width), out_shape=(sh...  15.8 us

profile of v3, /device:TPU:0, one launch (start us, length us, event | category | flops | bytes accessed | tf_op | source)
XLA Modules:
  0.0 344.4 jit_solution(6008180501998045046)
XLA Ops:
  0.0 0.0 copy-start
  0.7 0.6 pad_add_fusion.place_ref
  1.3 0.0 copy-done
  1.3 0.7 bitcast_bitcast_fusion.q_ref
  2.0 19.6 %gather_queries.1.q_ref = bf16[4,32,32,128]{3,2,1,0:T(8,128)(2,1)} custom-call(bf16[32,32,128]{2,1,0:T(8,128)(2,1)} %bitcast_bitcast_fusion.q_ref), custom_call_target="tpu_custom_call" | custom-call | tf_op jit(solution)/shard_map/gather_queries/pallas_call | solution.py:124
  21.7 28.3 %attend.1 = (f32[4,128,1024]{2,1,0:T(8,128)}, f32[8,1024]{1,0:T(8,128)}) custom-call(s32[3]{0:T(128)} %pad_add_fusion.place_ref, bf16[4,32,32,128]{3,2,1,0:T(8,128)(2,1)} %gather_queries.1.q_ref, bf16[3072,512]{1,0:T(8,128)(2,1)} %k_ref.1, bf16[3072,512]{1,0:T(8,128)(2,1)} %v_ref.1, bf16[32,512]{1,0:T(8,128)(2,1)} %nk_ref.1, bf16[32,512]{1,0:T(8,128)(2,1)} %nv_ref.1), custom_call_target="tpu_custom_call" | custom-call | tf_op jit(solution)/shard_map/attend/pallas_call | solution.py:199
  50.0 39.9 %merge.1 = bf16[4,32,32,128]{3,2,1,0:T(8,128)(2,1)} custom-call(f32[4,128,1024]{2,1,0:T(8,128)} %get-tuple-element.9.acc_ref, f32[8,1024]{1,0:T(8,128)} %get-tuple-element.10.st_ref), custom_call_target="tpu_custom_call" | custom-call | tf_op jit(solution)/shard_map/merge/pallas_call | solution.py:297
  89.9 1.6 copy.14
  91.5 5.7 %convolution_convert_fusion.p_ref = bf16[128,1024]{1,0:T(8,128)(2,1)} fusion(bf16[4096,1024]{1,0:T(8,128)(2,1)} %param.19, bf16[16,8,32,128]{3,2,1,0:T(8,128)(2,1)S(1)} %bitcast.25), kind=kOutput, calls=%fused_computation.4 | convolution fusion | flops 1073872896 | bytes 9699328 | tf_op jit(solution)/shard_map/dot_general | solution.py:579
  97.2 15.8 %norm.1 = (bf16[128,1024]{1,0:T(8,128)(2,1)}, bf16[128,1024]{1,0:T(8,128)(2,1)}) custom-call(bf16[128,1024]{1,0:T(8,128)(2,1)} %convolution_convert_fusion.p_ref, bf16[128,1024]{1,0:T(8,128)(2,1)} %r_ref.1, f32[1,1024]{1,0:T(1,128)} %bitcast.28), custom_call_target="tpu_custom_call" | custom-call | tf_op jit(solution)/shard_map/norm/pallas_call | solution.py:361
  113.1 0.0 copy-start.1
  113.1 19.6 %fusion.5.b_ref = bf16[2,128,7168]{2,1,0:T(8,128)(2,1)} fusion(bf16[1024,2,7168]{2,1,0:T(2,128)(2,1)} %param.20, bf16[128,1024]{1,0:T(8,128)(2,1)} %get-tuple-element.11), kind=kOutput, calls=%fused_computation.3 | convolution fusion | flops 3759931392 | bytes 33292288 | tf_op jit(solution)/shard_map/tk,ksn->stn/dot_general | solution.py:584
  132.7 210.0 %feed_forward.1 = bf16[64,1024]{1,0:T(8,128)(2,1)} custom-call(bf16[2,128,7168]{2,1,0:T(8,128)(2,1)} %fusion.5.b_ref, bf16[7168,1024]{1,0:T(8,128)(2,1)} %dn_hbm.1, bf16[2,64,1024]{2,1,0:T(8,128)(2,1)} %bitcast.27), custom_call_target="tpu_custom_call" | custom-call | tf_op jit(solution)/shard_map/feed_forward/pallas_call | solution.py:532
  342.8 1.6 copy.31
  344.4 0.0 copy-done.1
Async XLA Ops:
  0.0 1.3 copy-start
  113.1 231.3 %copy-start.1 = (bf16[32,4096]{1,0:T(8,128)(2,1)S(1)}, bf16[32,4096]{1,0:T(8,128)(2,1)}, u32[]{:S(2)}) copy-start(bf16[32,4096]{1,0:T(8,128)(2,1)} %param.11) | copy-start | bytes 786436

commit v4 on v1

--- a/solution.py
+++ b/solution.py
@@ -46,6 +46,64 @@
     return pltpu.CompilerParams(
         collective_id=collective_id, has_side_effects=True, vmem_limit_bytes=VMEM_LIMIT
     )
+
+
+def gather_line(o_ref, with_own, zs, zr, ks, kr):
+    n, me, _, _ = peers("ctx")
+    k = lax.axis_index("khalf")
+    sibling = {"khalf": 1 - k}
+    beside = ({"ctx": lax.rem(me + 1, n)}, {"ctx": lax.rem(me + n - 1, n)})
+    has_next = (me < n - 1, me > 0)
+    half = o_ref.shape[1] // 2
+    mine, other = pl.ds(k * half, half), pl.ds((1 - k) * half, half)
+
+    def pass_on(b, d):
+        block = o_ref.at[b, mine]
+        return remote(block, block, zs.at[d, b], zr.at[b], beside[d])
+
+    def across(b, part):
+        block = o_ref.at[b, part]
+        return remote(block, block, ks.at[b], kr.at[b], sibling)
+
+    for d in range(2):
+
+        @pl.when(has_next[d])
+        def _():
+            pass_on(me, d).start()
+
+    if with_own:
+        across(me, mine).start()
+    for hop in range(1, n):
+        for d in range(2):
+            b = me - hop if d == 0 else me + hop
+
+            @pl.when((b >= 0) & (b < n))
+            def _():
+                pass_on(b, d).wait_recv()
+
+                @pl.when(has_next[d])
+                def _():
+                    pass_on(b, d).start()
+
+                across(b, mine).start()
+
+    for b in range(n):
+
+        @pl.when(jnp.logical_or(with_own, me != b))
+        def _():
+            across(b, other).wait_recv()
+            across(b, mine).wait_send()
+
+        for d in range(2):
+
+            @pl.when(has_next[d] & ((b <= me) if d == 0 else (b >= me)))
+            def _():
+                pass_on(b, d).wait_send()
+
+
+def line_sems(n):
+    sem = pltpu.SemaphoreType.DMA
+    return [sem((2, n)), sem((n,)), sem((n,)), sem((n,))]
 
 
 def gather_queries_kernel(q_ref, o_ref, zs, zr, ks, kr, own):
@@ -142,9 +200,9 @@
     s = scored(nk_ref[...], usable)
     m, l, acc = update(state, s, usable, nv_ref[...])
     acc_ref[...] = acc[None]
-    st_ref[...] = jnp.zeros(st_ref.shape, jnp.float32)
-    st_ref[0, 0:1, :] = m
-    st_ref[0, 1:2, :] = l
+    group = pl.program_id(0)
+    st_ref[pl.ds(group, 1), :] = m
+    st_ref[pl.ds(group + st_ref.shape[0] // 2, 1), :] = l
 
 
 def attend(q_all, keys, values, new_keys, new_values, place):
@@ -160,7 +218,7 @@
         grid=(groups,),
         out_shape=(
             jax.ShapeDtypeStruct((groups, width, count), jnp.float32),
-            jax.ShapeDtypeStruct((groups, 8, count), jnp.float32),
+            jax.ShapeDtypeStruct((2 * groups, count), jnp.float32),
         ),
         in_specs=[
             pl.BlockSpec(memory_space=pltpu.SMEM),
@@ -172,7 +230,7 @@
         ],
         out_specs=(
             pl.BlockSpec((1, width, count), lambda g: (g, 0, 0)),
-            pl.BlockSpec((1, 8, count), lambda g: (g, 0, 0)),
+            pl.BlockSpec((2 * groups, count), lambda g: (0, 0)),
         ),
         compiler_params=pltpu.CompilerParams(vmem_limit_bytes=VMEM_LIMIT),
         name="attend",
@@ -182,7 +240,7 @@
 def merge_kernel(
     acc_ref, st_ref, o_ref,
     sib_st, chip_st, ctx_st, part, sib_part, mine_part, ctx_part,
-    s_st, r_st, s_z, r_z, s_p, r_p, s_a, r_a, s_g, r_g, s_k, r_k,
+    s_st, r_st, s_z, r_z, s_p, r_p, s_a, r_a, zs, zr, ks, kr,
 ):
     n, me, after, before = peers("ctx")
     k = lax.axis_index("khalf")
@@ -194,7 +252,7 @@
     half = heads // 2
 
     def stat_of(ref, at=()):
-        return ref[at + (slice(None), slice(0, 1))], ref[at + (slice(None), slice(1, 2))]
+        return ref[at + (slice(0, groups),)], ref[at + (slice(groups, 2 * groups),)]
 
     def joined(a, b):
         m = jnp.maximum(a[0], b[0])
@@ -205,9 +263,8 @@
     copy.wait()
     own = stat_of(st_ref)
     chip = joined(own, stat_of(sib_st))
-    chip_st[...] = jnp.zeros(chip_st.shape, jnp.float32)
-    chip_st[:, 0:1, :] = chip[0]
-    chip_st[:, 1:2, :] = chip[1]
+    chip_st[0:groups] = chip[0]
+    chip_st[groups : 2 * groups] = chip[1]
     copies = [
         remote(chip_st, ctx_st.at[i], s_z.at[i], r_z.at[i], {"ctx": c}) for i, c in enumerate(after)
     ]
@@ -219,43 +276,31 @@
         total = joined(total, stat_of(ctx_st, (i,)))
     factor = jnp.exp(own[0] - total[0]) / total[1]
     for g in range(groups):
-        scaled = jnp.transpose(acc_ref[g] * factor[g])
+        scaled = jnp.transpose(acc_ref[g] * factor[g : g + 1])
         part[:, g * size : (g + 1) * size] = scaled.reshape(n, size, rows, width).astype(part.dtype)
-    copy = remote(part.at[:, pl.ds((1 - k) * half, half)], sib_part, s_p, r_p, sibling)
-    copy.start()
-    copy.wait()
-    for c in range(n):
-        mine_part[c] = (
-            part[c, pl.ds(k * half, half)].astype(jnp.float32) + sib_part[c].astype(jnp.float32)
-        ).astype(part.dtype)
-    copies = [
-        remote(mine_part.at[c], ctx_part.at[i], s_a.at[i], r_a.at[i], {"ctx": c})
-        for i, c in enumerate(after)
-    ]
-    for copy in copies:
-        copy.start()
-    summed = mine_part[me].astype(jnp.float32)
-    for i, copy in enumerate(copies):
-        copy.wait()
-        summed = summed + ctx_part[i].astype(jnp.float32)
     mine = pl.ds(k * half, half)
     other = pl.ds((1 - k) * half, half)
+    swaps = [
+        remote(part.at[c, other], sib_part.at[c], s_p.at[i], r_p.at[i], sibling)
+        for i, c in enumerate(after + [me])
+    ]
+    meet_sums = []
+    for copy in swaps:
+        copy.start()
+    for i, c in enumerate(after + [me]):
+        swaps[i].wait_recv()
+        summed = part[c, mine].astype(jnp.float32) + sib_part[c].astype(jnp.float32)
+        if i < n - 1:
+            mine_part[c] = summed.astype(part.dtype)
+            copy = remote(mine_part.at[c], ctx_part.at[i], s_a.at[i], r_a.at[i], {"ctx": c})
+            copy.start()
+            meet_sums.append(copy)
+    for i, copy in enumerate(meet_sums):
+        copy.wait_recv()
+        summed = summed + ctx_part[i].astype(jnp.float32)
     o_ref[me, mine] = summed.astype(o_ref.dtype)
-    out = [
-        remote(o_ref.at[me, mine], o_ref.at[me, mine], s_g.at[i], r_g.at[i], {"ctx": c})
-        for i, c in enumerate(after)
-    ]
-    on = [remote(o_ref.at[me, mine], o_ref.at[me, mine], s_k.at[n - 1], r_k.at[n - 1], sibling)]
-    for copy in out + on:
-        copy.start()
-    for i, c in enumerate(before):
-        remote(o_ref.at[c, mine], o_ref.at[c, mine], s_g.at[i], r_g.at[i], sibling).wait_recv()
-        copy = remote(o_ref.at[c, mine], o_ref.at[c, mine], s_k.at[i], r_k.at[i], sibling)
-        copy.start()
-        on.append(copy)
-    for i, c in enumerate(before + [me]):
-        remote(o_ref.at[c, other], o_ref.at[c, other], s_k.at[i], r_k.at[i], sibling).wait_recv()
-    for copy in out + on:
+    gather_line(o_ref, True, zs, zr, ks, kr)
+    for copy in swaps + meet_sums:
         copy.wait_send()
 
 
@@ -275,7 +320,7 @@
             f32(*stats.shape), f32(*stats.shape), f32(max(n - 1, 1), *stats.shape),
             b16(n, heads, rows, width), b16(n, heads // 2, rows, width),
             b16(n, heads // 2, rows, width), b16(max(n - 1, 1), heads // 2, rows, width),
-            one, one, many, many, one, one, many, many, many, many, many, many,
+            one, one, many, many, many, many, many, many, *line_sems(n),
         ],
         compiler_params=params(1),
         name="merge",

time: 244 us -> 236 us (0.967)
  Pallas kernels: 118 us -> 112 us
    pallas_call x1, Pallas kernels: 47.4 us -> 41.9 us  [merge(): pl.pallas_call(merge_kernel, out_shape=jax.ShapeDtypeStruct((n, heads, ro...]
where the time goes in v4:
time: 236 us; the launch traced here: 235 us
  Pallas kernels  112 us (47%)
  waiting for transfers between devices  68.8 us (29%)
  matrix products  33.8 us (14%)
  between operations  14.2 us (6%)
  local copies, waits for them, and re-layouts  4.22 us (2%)
  other arithmetic  2.48 us (1%)
    reduce_scatter x1, waiting for transfers between devices, on_device(): lax.psum_scatter(both.astype(jnp.bfloat16), ('ctx', 'khalf'), scatter_dim...  43.4 us
    pallas_call x1, Pallas kernels, merge(): pl.pallas_call(merge_kernel, out_shape=jax.ShapeDtypeStruct((n, heads, ro...  41.9 us
    pallas_call x1, Pallas kernels, attend(): pl.pallas_call(functools.partial(attend_kernel, chunk), grid=(groups,), o...  28.3 us
    all_gather x1, waiting for transfers between devices, on_device(): lax.all_gather(activated, ('ctx', 'khalf'), axis=0, tiled=True)  25.4 us
    dot_general x1, matrix products, on_device(): jnp.einsum('tk,ksn->tsn', normed, gate_up, preferred_element_type=jnp.flo...  19.6 us
    pallas_call x1, Pallas kernels, gather_queries(): pl.pallas_call(gather_queries_kernel, out_shape=jax.ShapeDtypeStruct((n,)...  18.2 us
    pallas_call x1, Pallas kernels, norm(): pl.pallas_call(functools.partial(norm_kernel, total_width), out_shape=(sh...  15.8 us
    dot_general x1, matrix products, on_device(): jnp.dot(lax.all_gather(activated, ('ctx', 'khalf'), axis=0, tiled=True),...  8.5 us
  transfers between devices with their start and end apart: 2, of which 2 were waited for; matrix products, arithmetic and copies ran while one was open for 0% of the time, Pallas kernels for 0%

profile of v4, /device:TPU:0, one launch (start us, length us, event | category | flops | bytes accessed | tf_op | source)
XLA Modules:
  0.0 235.2 jit_solution(676368821948863618)
XLA Ops:
  6.5 0.0 copy-start
  6.5 0.0 reduce-scatter.2.cloned.1.call-start
  7.2 0.3 copy-done
  7.5 0.7 bitcast_bitcast_fusion.q_ref
  8.2 18.2 %gather_queries.1.q_ref = bf16[4,32,32,128]{3,2,1,0:T(8,128)(2,1)} custom-call(bf16[32,32,128]{2,1,0:T(8,128)(2,1)} %bitcast_bitcast_fusion.q_ref), custom_call_target="tpu_custom_call" | custom-call | tf_op jit(solution)/shard_map/gather_queries/pallas_call | solution.py:141
  26.5 0.6 pad_add_fusion.place_ref
  27.1 28.3 %attend.1 = (f32[4,128,1024]{2,1,0:T(8,128)}, f32[8,1024]{1,0:T(8,128)}) custom-call(s32[3]{0:T(128)} %pad_add_fusion.place_ref, bf16[4,32,32,128]{3,2,1,0:T(8,128)(2,1)} %gather_queries.1.q_ref, bf16[3072,512]{1,0:T(8,128)(2,1)} %k_ref.1, bf16[3072,512]{1,0:T(8,128)(2,1)} %v_ref.1, bf16[32,512]{1,0:T(8,128)(2,1)} %nk_ref.1, bf16[32,512]{1,0:T(8,128)(2,1)} %nv_ref.1), custom_call_target="tpu_custom_call" | custom-call | tf_op jit(solution)/shard_map/attend/pallas_call | solution.py:216
  55.4 41.9 %merge.1 = bf16[4,32,32,128]{3,2,1,0:T(8,128)(2,1)} custom-call(f32[4,128,1024]{2,1,0:T(8,128)} %get-tuple-element.9.acc_ref, f32[8,1024]{1,0:T(8,128)} %get-tuple-element.10.st_ref), custom_call_target="tpu_custom_call" | custom-call | tf_op jit(solution)/shard_map/merge/pallas_call | solution.py:314
  97.3 1.6 copy.14
  98.9 5.7 %convolution_convert_fusion.p_ref = bf16[128,1024]{1,0:T(8,128)(2,1)} fusion(bf16[4096,1024]{1,0:T(8,128)(2,1)} %param.19, bf16[16,8,32,128]{3,2,1,0:T(8,128)(2,1)S(1)} %bitcast.36), kind=kOutput, calls=%fused_computation.3 | convolution fusion | flops 1073872896 | bytes 9699328 | tf_op jit(solution)/shard_map/dot_general | solution.py:453
  104.7 15.8 %norm.1 = (bf16[128,1024]{1,0:T(8,128)(2,1)}, bf16[128,1024]{1,0:T(8,128)(2,1)}) custom-call(bf16[128,1024]{1,0:T(8,128)(2,1)} %convolution_convert_fusion.p_ref, bf16[128,1024]{1,0:T(8,128)(2,1)} %r_ref.1, f32[1,1024]{1,0:T(1,128)} %bitcast.40), custom_call_target="tpu_custom_call" | custom-call | tf_op jit(solution)/shard_map/norm/pallas_call | solution.py:378
  120.5 19.6 %fusion.2 = bf16[128,2,7168]{2,0,1:T(8,128)(2,1)} fusion(bf16[1024,2,7168]{2,1,0:T(2,128)(2,1)} %param.20, bf16[128,1024]{1,0:T(8,128)(2,1)} %get-tuple-element.11), kind=kOutput, calls=%fused_computation.2 | convolution fusion | flops 3759931392 | bytes 33292288 | tf_op jit(solution)/shard_map/tk,ksn->tsn/dot_general | solution.py:458
  140.1 0.0 reduce-scatter.2.cloned.1.call-update
  140.1 0.0 all-gather.2.cloned.1.call-start
  140.2 43.4 %reduce-scatter.2.cloned.1.call-done = bf16[16,2,7168]{2,0,1:T(8,128)(2,1)} async-done(((bf16[128,2,7168]{2,0,1:T(8,128)(2,1)}), bf16[16,2,7168]{2,0,1:T(8,128)(2,1)}) %reduce-scatter.2.cloned.1.call-update) | async-done | bytes 458768 | tf_op jit(solution)/shard_map/reduce_scatter | solution.py:459
  183.5 1.1 convert_element_type.17
  184.6 0.8 fusion.8
  185.4 0.0 all-gather.2.cloned.1.call-update
  185.4 0.0 copy-start.1
  185.5 25.4 %all-gather.2.cloned.1.call-done = bf16[128,7168]{1,0:T(8,128)(2,1)} async-done(((bf16[16,7168]{1,0:T(8,128)(2,1)}), bf16[128,7168]{1,0:T(8,128)(2,1)}) %all-gather.2.cloned.1.call-update) | async-done | bytes 1835024 | tf_op jit(solution)/shard_map/all_gather | solution.py:464
  210.9 8.5 %convolution_convert_fusion.1 = bf16[128,1024]{1,0:T(8,128)(2,1)} fusion(bf16[128,7168]{1,0:T(8,128)(2,1)} %all-gather.2.cloned.1.call-done, bf16[7168,1024]{1,0:T(8,128)(2,1)} %param.21), kind=kOutput, calls=%fused_computation.4 | convolution fusion | flops 1879179264 | bytes 16777216 | tf_op jit(solution)/shard_map/dot_general | solution.py:463
  219.4 7.4 %finish.1 = bf16[64,1024]{1,0:T(8,128)(2,1)} custom-call(bf16[2,64,1024]{2,1,0:T(8,128)(2,1)} %bitcast.38, bf16[2,64,1024]{2,1,0:T(8,128)(2,1)} %bitcast.39), custom_call_target="tpu_custom_call" | custom-call | tf_op jit(solution)/shard_map/finish/pallas_call | solution.py:414
  226.8 1.6 copy.29
  228.3 0.0 copy-done.1
Async XLA Ops:
  6.5 1.0 copy-start
  6.5 177.0 %reduce-scatter.2.cloned.1.call-start = ((), (), s32[]{:S(2)}) async-start(), calls=%async_computation.1 | async-start | bytes 4128768 | tf_op jit(solution)/shard_map/reduce_scatter | solution.py:459
  140.1 70.8 %all-gather.2.cloned.1.call-start = ((), (), s32[]{:S(2)}) async-start(), calls=%async_computation.2 | async-start | bytes 2064384 | tf_op jit(solution)/shard_map/all_gather | solution.py:464
  185.4 42.9 %copy-start.1 = (bf16[32,4096]{1,0:T(8,128)(2,1)S(1)}, bf16[32,4096]{1,0:T(8,128)(2,1)}, u32[]{:S(2)}) copy-start(bf16[32,4096]{1,0:T(8,128)(2,1)} %param.11) | copy-start | bytes 786436
Sparse Core Ops, SparseCore 0:
  140.2 43.2 reduce-scatter.1
  185.6 25.2 all-gather.1
